TPU v7x, 32 devices: a whole 2x2x4 slice. The times are simulated.
32 devices in a mesh: ctx: 8 (over z, y), head: 4 (over x, core).
Axes of the slice: x: 2, y: 2, z: 4, core: 2. Of those that a mesh axis runs over, the one named last changes fastest.
Arguments:
- queries: bfloat16 [4096, 5120], P('ctx', 'head'), may hold values from -34 to 34
- key_rows: bfloat16 [4096, 5120], P('ctx', 'head'), may hold values from -8 to 8
- value_rows: bfloat16 [4096, 5120], P('ctx', 'head'), may hold values from -23 to 23
- learning_rates: float32 [8, 4096], P('head', 'ctx'), may hold values from 0.02 to 1
- fast_gate: bfloat16 [8, 640, 640], P('head'), may hold values from -0.25 to 0.25
- fast_lift: bfloat16 [8, 640, 640], P('head'), may hold values from -0.25 to 0.25
- fast_down: bfloat16 [8, 640, 640], P('head'), may hold values from -0.25 to 0.25
- output_gain: float32 [5120], P('head'), may hold values from 0.25 to 1.75
- output_weight: bfloat16 [5120, 5120], P(None, 'head'), may hold values from -0.078125 to 0.078125
Outputs:
- layer_output: bfloat16 [4096, 5120], P('ctx', 'head')
All inputs are finite; a program needn't handle non-finite values.
Results may differ from a plain program's by a relative error of at most 0.025.
Values may be sent and summed in bfloat16 or wider, within the bound.
No kernel may reach another device: no remote copies, remote signals or barrier semaphores. Data moves between devices by JAX's collectives and lax.ppermute only.
A program may use at most 128 MiB of HBM per device.

v0:
```python
import functools
import math

import jax
import jax.numpy as jnp
from jax import lax
from jax.experimental import pallas as pl
from jax.experimental.pallas import tpu as pltpu
from jax.sharding import PartitionSpec as P

ATT_HD = 128
WINDOW = 512
NS_ITERS = 3
PIECES = 2
VMEM_BYTES = 20 * 1024 * 1024
PROJECT_BYTES = 28 * 1024 * 1024

quintic_first = 3.4445
quintic_second = -4.775
quintic_third = 2.0315

f32 = jnp.float32
bf16 = jnp.bfloat16


def mm(a, b, dims=((1,), (0,))):
    return lax.dot_general(a, b, (dims, ((), ())), preferred_element_type=f32)


def after(value, *earlier):
    return lax.optimization_barrier((value, *earlier))[0]


def pick(blocks, which):
    out = blocks[0]
    for number in range(1, len(blocks)):
        out = jnp.where(which == number, blocks[number], out)
    return out


def tree_low(low, high):
    levels, step = [], 1
    while step < high - low:
        levels.append(
            [(i + step, i) for i in range(low, high, 2 * step) if i + step < high]
        )
        step *= 2
    return levels


def tree_high(low, high):
    return [
        [(low + high - 1 - a, low + high - 1 - b) for a, b in level]
        for level in tree_low(low, high)
    ]


def tree_ends(count):
    low = tree_low(0, count // 2)
    return [
        [(2 * a, 2 * b) for a, b in level]
        + [(count - 1 - 2 * a, count - 1 - 2 * b) for a, b in level]
        for level in low
    ]


def tree_mid(count):
    middle = count // 2
    left, right = tree_high(0, middle), tree_low(middle, count)
    levels = []
    for k in range(max(len(left), len(right))):
        levels.append((left[k] if k < len(left) else []) + (right[k] if k < len(right) else []))
    return levels + [[(middle, middle - 1)]]


def spread_ends(count):
    levels, step = [], count // 2
    while step > 1:
        low = [(i, i + step) for i in range(0, count, 2 * step)]
        levels.append(low + [(count - 1 - a, count - 1 - b) for a, b in low])
        step //= 2
    return levels


def attention_kernel(first_ref, q_ref, kp_ref, k_ref, vp_ref, v_ref, out_ref, k_all, v_turned):
    tokens = q_ref.shape[0]
    tile = ATT_HD
    span = WINDOW + tile
    k_all[:WINDOW] = kp_ref[...]
    k_all[WINDOW:] = k_ref[...]
    v_turned[:, :WINDOW] = vp_ref[...].T
    v_turned[:, WINDOW:] = v_ref[...].T
    is_first = first_ref[0] == 0
    key = lax.broadcasted_iota(jnp.int32, (tile, tile), 0)
    query = lax.broadcasted_iota(jnp.int32, (tile, tile), 1)
    scale = ATT_HD**-0.5 * math.log2(math.e)
    for number in range(tokens // tile):
        start = number * tile
        s = mm(k_all[start : start + span], q_ref[start : start + tile], ((1,), (1,)))
        inner = s[tile:WINDOW]
        head_rows = key > query
        if start < WINDOW:
            head_rows = head_rows & jnp.logical_not(is_first)
            place = start + tile + lax.broadcasted_iota(jnp.int32, inner.shape, 0)
            inner = jnp.where((place >= WINDOW) | jnp.logical_not(is_first), inner, -1e30)
        s = jnp.concatenate(
            [
                jnp.where(head_rows, s[:tile], -1e30),
                inner,
                jnp.where(key <= query, s[WINDOW:], -1e30),
            ]
        )
        peak = jnp.max(s, axis=0, keepdims=True)
        w = jnp.exp2((s - peak) * scale)
        total = jnp.sum(w, axis=0, keepdims=True)
        o = mm(v_turned[:, start : start + span], w.astype(bf16))
        out_ref[start : start + tile] = (o / total).T


def attention(q, kp, k, vp, v, plane):
    tokens, width = q.shape
    wide = pl.BlockSpec((tokens, ATT_HD), lambda a, s: (0, a))
    before = pl.BlockSpec((WINDOW, ATT_HD), lambda a, s: (0, a))
    return pl.pallas_call(
        attention_kernel,
        out_shape=jax.ShapeDtypeStruct((tokens, width), f32),
        grid_spec=pltpu.PrefetchScalarGridSpec(
            num_scalar_prefetch=1,
            grid=(width // ATT_HD,),
            in_specs=[wide, before, wide, before, wide],
            out_specs=wide,
            scratch_shapes=[
                pltpu.VMEM((WINDOW + tokens, ATT_HD), bf16),
                pltpu.VMEM((ATT_HD, WINDOW + tokens), bf16),
            ],
        ),
        compiler_params=pltpu.CompilerParams(vmem_limit_bytes=VMEM_BYTES),
        cost_estimate=pl.CostEstimate(
            flops=4 * tokens * (WINDOW + ATT_HD) * width,
            bytes_accessed=12 * tokens * width,
            transcendentals=tokens * (WINDOW + ATT_HD) * (width // ATT_HD),
        ),
    )(jnp.reshape(plane, (1,)).astype(jnp.int32), q, kp, k, vp, v)


def settle_kernel(active_ref, grad_ref, init_ref, out_ref, x_ref):
    @pl.when(active_ref[0] == 1)
    def _():
        g = grad_ref[...]
        square = jnp.sum(jnp.sum(g * g, axis=0, keepdims=True), axis=1, keepdims=True)
        x_ref[...] = (g / (jnp.sqrt(square) + 1e-06)).astype(bf16)

        for _ in range(NS_ITERS):
            x = x_ref[...]
            gram = mm(x, x, ((1,), (1,))).astype(bf16)
            product = mm(gram, x).astype(bf16)
            second = mm(gram, product)
            x_ref[...] = (
                quintic_first * x.astype(f32)
                + quintic_second * product.astype(f32)
                + quintic_third * second
            ).astype(bf16)

        initial = init_ref[...].astype(f32)
        updated = initial + x_ref[...].astype(f32)
        target = jnp.sqrt(jnp.sum(initial * initial, axis=0, keepdims=True))
        current = jnp.sqrt(jnp.sum(updated * updated, axis=0, keepdims=True) + 1e-06)
        out_ref[...] = (updated * (target / current)).astype(bf16)

    @pl.when(active_ref[0] == 0)
    def _():
        out_ref[...] = jnp.zeros_like(out_ref)


def renew(gradient, initial, active):
    rows, columns = gradient.shape
    vmem = pl.BlockSpec(memory_space=pltpu.VMEM)
    return pl.pallas_call(
        settle_kernel,
        out_shape=jax.ShapeDtypeStruct((rows, columns), bf16),
        in_specs=[pl.BlockSpec(memory_space=pltpu.SMEM), vmem, vmem],
        out_specs=vmem,
        scratch_shapes=[pltpu.VMEM((rows, columns), bf16)],
        compiler_params=pltpu.CompilerParams(vmem_limit_bytes=VMEM_BYTES),
        cost_estimate=pl.CostEstimate(
            flops=6 * NS_ITERS * rows * rows * columns,
            bytes_accessed=8 * rows * columns,
            transcendentals=0,
        ),
    )(jnp.reshape(active, (1,)).astype(jnp.int32), gradient, initial)


def apply_kernel(which_ref, q_ref, gate_ref, lift_ref, down_ref, att_ref, gain_ref, *out_refs):
    q = q_ref[...]
    gate = mm(q, gate_ref[...])
    lift = mm(q, lift_ref[...])
    hidden = (gate / (1.0 + jnp.exp(-gate)) * lift).astype(bf16)
    result = mm(hidden, down_ref[...])
    scale = lax.rsqrt(jnp.mean(result * result, axis=1, keepdims=True) + 1e-06)
    combined = (att_ref[...] + result * scale * gain_ref[...]).astype(bf16)
    for number, out_ref in enumerate(out_refs):

        @pl.when(pl.program_id(0) == number)
        def _(out_ref=out_ref):
            out_ref[...] = combined


def apply_fast(q, gate, lift, down, attended, gain, order):
    rows, width = q.shape
    count = len(order)
    tokens = rows // count
    whole = pl.BlockSpec((width, width), lambda i, s: (0, 0))
    picked = pl.BlockSpec((tokens, width), lambda i, s: (s[i], 0))
    return pl.pallas_call(
        apply_kernel,
        out_shape=[jax.ShapeDtypeStruct((tokens, width), bf16)] * count,
        grid_spec=pltpu.PrefetchScalarGridSpec(
            num_scalar_prefetch=1,
            grid=(count,),
            in_specs=[picked, whole, whole, whole, picked, pl.BlockSpec((1, width), lambda i, s: (0, 0))],
            out_specs=[pl.BlockSpec((tokens, width), lambda i, s: (0, 0))] * count,
        ),
        compiler_params=pltpu.CompilerParams(vmem_limit_bytes=VMEM_BYTES),
        cost_estimate=pl.CostEstimate(
            flops=6 * rows * width * width,
            bytes_accessed=10 * rows * width + 6 * width * width,
            transcendentals=rows * width,
        ),
    )(jnp.stack(order).astype(jnp.int32), q, gate, lift, down, attended, gain)


def project_kernel(origins, group, has_total, spot_ref, w_ref, *refs):
    count = len(origins)
    chunk_refs = refs[:count]
    total_ref = refs[count] if has_total else None
    out_ref, joined, w_rows, arrived = refs[-4:]
    depth = chunk_refs[0].shape[1]
    copies = []
    for number, (offset, head) in enumerate(origins):
        start = ((spot_ref[0] ^ offset) * group + spot_ref[1 + head]) * depth
        copy = pltpu.make_async_copy(
            w_ref.at[pl.ds(pl.multiple_of(start, depth), depth)],
            w_rows.at[pl.ds(number * depth, depth)],
            arrived.at[number],
        )
        copy.start()
        copies.append(copy)
    for number in range(count):
        joined[:, number * depth : (number + 1) * depth] = chunk_refs[number][...]
    for copy in copies:
        copy.wait()
    tile = math.gcd(out_ref.shape[1], 256)

    @pl.loop(0, out_ref.shape[1] // tile)
    def _(number):
        at = pl.ds(pl.multiple_of(number * tile, tile), tile)
        result = mm(joined[...], w_rows[:, at])
        if has_total:
            result += total_ref[:, at]
        out_ref[:, at] = result.astype(out_ref.dtype)


def project(parts, group, spot, weight, total, is_last):
    chunks, origins = [part[0] for part in parts], [part[1:] for part in parts]
    count = len(chunks)
    rows, depth = chunks[0].shape
    columns = weight.shape[1]
    vmem = pl.BlockSpec(memory_space=pltpu.VMEM)
    operands = [spot, weight] + list(chunks) + ([] if total is None else [total])
    return pl.pallas_call(
        functools.partial(project_kernel, origins, group, total is not None),
        out_shape=jax.ShapeDtypeStruct((rows, columns), bf16 if is_last else f32),
        in_specs=[pl.BlockSpec(memory_space=pltpu.SMEM), pl.BlockSpec(memory_space=pltpu.HBM)]
        + [vmem] * (len(operands) - 2),
        out_specs=vmem,
        scratch_shapes=[
            pltpu.VMEM((rows, count * depth), bf16),
            pltpu.VMEM((count * depth, columns), bf16),
            pltpu.SemaphoreType.DMA((count,)),
        ],
        compiler_params=pltpu.CompilerParams(vmem_limit_bytes=PROJECT_BYTES),
        cost_estimate=pl.CostEstimate(
            flops=16 * count * rows * depth * columns,
            bytes_accessed=2 * count * (rows + columns) * depth + 8 * rows * columns,
            transcendentals=0,
        ),
    )(*operands)


OVER_TOKENS = ((0,), (0,))


def forward(keys, gate, lift):
    gate_pre = mm(keys, gate)
    lift_pre = mm(keys, lift)
    logistic = jax.nn.sigmoid(gate_pre)
    silu = gate_pre * logistic
    hidden = (silu * lift_pre).astype(bf16)
    return hidden, lift_pre * (logistic * (1.0 + gate_pre * (1.0 - logistic))), silu


def on_device(
    queries,
    key_rows,
    value_rows,
    learning_rates,
    fast_gate,
    fast_lift,
    fast_down,
    output_gain,
    output_weight,
):
    tokens = queries.shape[0]
    group, width = fast_gate.shape[0], fast_gate.shape[1]
    context = lax.axis_size("ctx")
    columns_of = lax.axis_size("head")
    planes = context // group
    place = lax.axis_index("ctx")
    member, plane = place % group, place // group
    head_place = lax.axis_index("head")

    def to_member(array, by):
        pairs = [(i, i // group * group + (i + by) % group) for i in range(context)]
        return lax.ppermute(array, "ctx", pairs)

    def between_planes(array, pairs):
        return lax.ppermute(
            array,
            "ctx",
            [(a * group + m, b * group + m) for a, b in pairs for m in range(group)],
        )

    def by_side(array, pairs):
        moves = []
        for h in range(columns_of):
            for a, b in pairs:
                a, b = (a, b) if h % 2 == 0 else (planes - 1 - a, planes - 1 - b)
                moves += [
                    ((a * group + m) * columns_of + h, (b * group + m) * columns_of + h) for m in range(group)
                ]
        return lax.ppermute(array, ("ctx", "head"), moves)

    def head_columns(array, by):
        return lax.dynamic_slice_in_dim(array, (member + by) % group * width, width, 1)

    gate, lift, down = (
        lax.dynamic_index_in_dim(w, member, 0, keepdims=False)
        for w in (fast_gate, fast_lift, fast_down)
    )
    gain = lax.dynamic_slice_in_dim(output_gain, member * width, width, 0)[None]

    onward = [(i, i + 1) for i in range(planes - 1)]

    def in_order(blocks):
        return [pick(blocks, (member - j) % group) for j in range(group)]

    keys = [head_columns(key_rows, by) for by in range(group)]
    values = [head_columns(value_rows, by) for by in range(group)]
    asked = [head_columns(queries, by) for by in range(group)]
    rates = [
        lax.dynamic_index_in_dim(learning_rates, (member + by) % group, 0, keepdims=False)
        for by in range(group)
    ]
    sent_keys = keys[-1]
    keys = keys[:1] + [to_member(keys[by], by) for by in range(1, group)]
    rates = rates[:1] + [to_member(after(rates[by], sent_keys), by) for by in range(1, group)]
    values = values[:1] + [to_member(values[by], by) for by in range(1, group)]
    ordered_keys = in_order(keys)
    earlier_keys = between_planes(ordered_keys[-1][-WINDOW:], onward)
    forwards = [forward(block, gate, lift) for block in keys]
    hidden = forwards[-1][0]
    values = values[:1] + [after(block, hidden) for block in values[1:]]

    hiddens, slopes, silus, scaleds = [], [], [], []
    total_down = 0.0
    for by in range(group):
        hidden, slope, silu = forwards[by]
        scaled = (rates[by][:, None] * values[by].astype(f32)).astype(bf16)
        total_down = total_down + mm(hidden, scaled, OVER_TOKENS)
        slopes.append(slope)
        silus.append(silu)
        scaleds.append(scaled)
    total_gate, total_lift = 0.0, 0.0
    for by in range(group):
        scaled = scaleds[by] if by < group - 1 else after(scaleds[by], total_down, earlier_keys)
        backward = mm(scaled, down, ((1,), (1,)))
        total_gate = total_gate + mm(keys[by], (backward * slopes[by]).astype(bf16), OVER_TOKENS)
        total_lift = total_lift + mm(keys[by], (backward * silus[by]).astype(bf16), OVER_TOKENS)

    ordered_values = in_order([after(block, backward) for block in values])
    window_values = ordered_values[-1][-WINDOW:]
    values_early = between_planes(window_values, onward[1:])

    rows = width // PIECES

    def cut(matrix):
        return [matrix[piece * rows : (piece + 1) * rows] for piece in range(PIECES)]

    def add_from(own, pairs):
        return own + between_planes(own.astype(bf16), pairs).astype(f32)

    down_levels = tree_mid(planes)
    side_plane = jnp.where(head_place % 2 == 0, plane, planes - 1 - plane)

    def add_side(own, pairs):
        return own + by_side(own.astype(bf16), pairs).astype(f32)

    sum_down = add_side(total_down, down_levels[0])
    asked = asked[:1] + [to_member(after(asked[by], sum_down), by) for by in range(1, group)]
    odd = plane % 2 == 1
    kept = jnp.where(odd, total_lift, total_gate)
    given = jnp.where(odd, total_gate, total_lift).astype(bf16)
    neighbours = [(i, i ^ 1) for i in range(planes)]
    given = between_planes(after(given, sum_down, values_early), neighbours)
    first_sum = sum_down
    for level in down_levels[1:]:
        sum_down = add_side(sum_down, level)
    kept = kept + given.astype(f32)
    met = [kept]
    values_first = between_planes(after(window_values, first_sum), onward[:1])
    earlier_values = jnp.where(plane == 1, values_first, values_early)
    middle_plane = side_plane == planes // 2 - 1
    new_down = renew(after(sum_down, values_first, *met), down, middle_plane)
    for level in tree_ends(planes):
        kept = after(kept, new_down) + between_planes(kept.astype(bf16), level).astype(f32)

    def spread(own, pairs):
        got = between_planes(own, pairs)
        here = functools.reduce(jnp.logical_or, [plane == b for _, b in pairs])
        return jnp.where(here, got, own)

    low_plane, high_plane = plane == 0, plane == planes - 1
    new_sums = kept
    new_outer = renew(after(new_sums, new_down), jnp.where(low_plane, gate, lift), low_plane | high_plane)
    owned_down, owner = after(new_down, new_sums), planes // 2 - 1
    passed_on = []
    for level in reversed(down_levels):
        from_owner = [(b, a) for a, b in level if b == owner]
        got = by_side(owned_down, from_owner)
        here = functools.reduce(jnp.logical_or, [side_plane == b for _, b in from_owner])
        new_down = jnp.where(here, got, new_down)
        passed_on.append([(b, a) for a, b in level if b != owner])
    far_levels = spread_ends(planes)
    from_ends = [(i, i ^ 1) for i in (0, planes - 1)]
    from_others = [(i, i ^ 1) for i in range(1, planes - 1)]
    near, passed_by = [], []
    for own in cut(new_outer):
        passed = own
        for level in far_levels:
            got = between_planes(own, level)
            here = functools.reduce(jnp.logical_or, [plane == b for _, b in level])
            own = jnp.where(here, got, own)
            passed = got
        near.append(own)
        passed_by.append(passed if len(far_levels) == 1 else own)
    other_ends = between_planes(after(new_outer, passed_by[0]), from_ends)
    others = jnp.concatenate([between_planes(passed, from_others) for passed in passed_by])
    beside_end = (plane == 1) | (plane == planes - 2)
    for pairs in passed_on:
        if pairs:
            got = by_side(after(new_down, near[0]), pairs)
            here = functools.reduce(jnp.logical_or, [side_plane == b for _, b in pairs])
            new_down = jnp.where(here, got, new_down)

    all_asked = jnp.concatenate(in_order(asked))
    attended = attention(
        after(all_asked, *near),
        earlier_keys,
        jnp.concatenate(ordered_keys),
        earlier_values,
        jnp.concatenate(ordered_values),
        plane,
    )
    other = jnp.where(beside_end, after(other_ends, attended), after(others, attended))
    mine, even = jnp.concatenate(near), plane % 2 == 0
    new_gate, new_lift = jnp.where(even, mine, other), jnp.where(even, other, mine)

    bits = [1 << k for k in reversed(range(columns_of.bit_length() - 1))]

    def swapped(part, bit):
        return lax.ppermute(part, "head", [(i, i ^ bit) for i in range(columns_of)])

    turns = list(range(1, group)) + [0]
    combined = apply_fast(
        all_asked, new_gate, new_lift, new_down, attended, gain, [(member - by) % group for by in turns]
    )
    arrived = [
        (to_member(rows_of, group - by), (member + by) % group) for by, rows_of in zip(turns[:-1], combined)
    ]
    combined = combined[-1]
    arrived = [(combined, member)] + arrived

    spot = jnp.stack([head_place] + [head for _, head in arrived]).astype(jnp.int32)
    parts = [(chunk, 0, number) for number, (chunk, _) in enumerate(arrived)]
    parts += [(swapped(chunk, bits[0]), bits[0], number) for number, (chunk, _) in enumerate(arrived)]
    total = project(parts[:-1], group, spot, output_weight, None, False)
    last, offset, number = parts[-1]
    parts[-1] = (after(last, total), offset, number)
    copies = [(after(part, parts[-1][0]), o, n) for part, o, n in parts]
    for bit in bits[1:]:
        copies += [(swapped(part, bit), o ^ bit, n) for part, o, n in copies]
    total = project(parts[-1:], group, spot, output_weight, total, False)
    return project(copies[len(parts) :], group, spot, output_weight, total, True)


def solution(mesh):
    return jax.shard_map(
        on_device,
        mesh=mesh,
        in_specs=(
            P("ctx", "head"),
            P("ctx", "head"),
            P("ctx", "head"),
            P("head", "ctx"),
            P("head", None, None),
            P("head", None, None),
            P("head", None, None),
            P("head"),
            P(None, "head"),
        ),
        out_specs=P("ctx", "head"),
        check_vma=False,
    )
```

profile of v0, /device:TPU:0, one launch (start us, length us, event | category | flops | bytes accessed | tf_op | source)
XLA Modules:
  0.0 191.2 jit_solution(9062510741725804938)
XLA Ops:
  2.2 3.0 %collective-permute-start = (bf16[512,640]{1,0:T(8,128)(2,1)}, bf16[512,640]{1,0:T(8,128)(2,1)}, u32[]{:S(2)}, u32[]{:S(2)}) collective-permute-start(bf16[512,640]{1,0:T(8,128)(2,1)} %constant_dynamic-slice_fusion.2), channel_id=1, source_target_pairs={{0,4},{4,0},{8,12},{12,8},{16,20},{20,16},{24,28},{28,24},{1,5},{5... | collective-permute-start | bytes 1966088 | tf_op jit(solution)/shard_map/ppermute | solution.py:324
  5.2 2.2 %constant_dynamic-slice_fusion = (bf16[512,640]{1,0:T(8,128)(2,1)}, bf16[512,640]{1,0:T(8,128)(2,1)S(1)}) fusion(bf16[512,1280]{1,0:T(8,128)(2,1)} %param.11, s32[]{:T(128)S(6)} %select_n.197, s32[]{:T(128)S(6)} %select_n.198), kind=kLoop, calls=%fused_computation.65 | loop fusion | bytes 2621448 | tf_op jit(solution)/shard_map/dynamic_slice | solution.py:344
  17.0 4.0 %collective-permute-done = bf16[512,640]{1,0:T(8,128)(2,1)} collective-permute-done((bf16[512,640]{1,0:T(8,128)(2,1)}, bf16[512,640]{1,0:T(8,128)(2,1)}, u32[]{:S(2)}, u32[]{:S(2)}) %collective-permute-start) | collective-permute-done | bytes 655392 | tf_op jit(solution)/shard_map/ppermute | solution.py:324
  21.0 2.2 %broadcast_select_fusion.9 = (bf16[512,640]{1,0:T(8,128)(2,1)}, bf16[512,640]{1,0:T(8,128)(2,1)S(1)}) fusion(bf16[512,640]{1,0:T(8,128)(2,1)} %collective-permute-done, pred[]{:T(512)S(6)} %eq.70, bf16[512,1280]{1,0:T(8,128)(2,1)S(1)} %copy-done.3, s32[]{:T(128)S(6)} %select_n.198, pred[]{:T(512)S(6)} %eq.71), kind=kLoop, calls=%fused_computation.48 | loop fusion | flops 655360 | bytes 2621446 | tf_op jit(solution)/shard_map/jit(_where)/select_n | solution.py:37
  23.2 4.1 %collective-permute-start.5 = (bf16[512,640]{1,0:T(8,128)(2,1)S(1)}, bf16[512,640]{1,0:T(8,128)(2,1)S(1)}, u32[]{:S(2)}, u32[]{:S(2)}) collective-permute-start(bf16[512,640]{1,0:T(8,128)(2,1)S(1)} %get-tuple-element.60), channel_id=1, source_target_pairs={{0,8},{4,12},{8,16},{12,20},{16,24},{20,28},{1,9},{5,13},{9,17},{1... | collective-permute-start | bytes 1966088 | tf_op jit(solution)/shard_map/ppermute | solution.py:327
  31.0 3.3 %collective-permute-done.2 = bf16[512,640]{1,0:T(8,128)(2,1)} collective-permute-done((bf16[512,640]{1,0:T(8,128)(2,1)}, bf16[512,640]{1,0:T(8,128)(2,1)}, u32[]{:S(2)}, u32[]{:S(2)}) %collective-permute-start.2) | collective-permute-done | bytes 655392 | tf_op jit(solution)/shard_map/ppermute | solution.py:324
  36.2 3.8 %collective-permute-start.3 = (bf16[640,640]{1,0:T(8,128)(2,1)S(1)}, bf16[640,640]{1,0:T(8,128)(2,1)S(1)}, u32[]{:S(2)}, u32[]{:S(2)}) collective-permute-start(bf16[640,640]{1,0:T(8,128)(2,1)S(1)} %get-tuple-element.73), channel_id=1, source_target_pairs={{0,8},{4,12},{24,16},{28,20},{25,17},{29,21},{1,9},{5,13},{2,10},{... | collective-permute-start | bytes 2457608 | tf_op jit(solution)/shard_map/ppermute | solution.py:341
  45.6 3.9 %select_convert_fusion = (bf16[640,640]{1,0:T(8,128)(2,1)}, f32[640,640]{1,0:T(8,128)}) fusion(f32[640,640]{1,0:T(8,128)S(1)} %convolution_add_fusion.1, pred[]{:T(512)S(6)} %eq.77, f32[640,640]{1,0:T(8,128)S(1)} %fusion.13, bf16[512,640]{1,0:T(8,128)(2,1)} %collective-permute-done, f32[512,640]{1,0:T(8,128)S(1)} %fusion.40, ...), kind=kOutput, calls=%fused_computation.3 | convolution fusion | flops 423526400 | bytes 10321921 | tf_op jit(solution)/shard_map/dot_general | solution.py:27
  49.5 7.2 %collective-permute-done.3 = bf16[640,640]{1,0:T(8,128)(2,1)S(1)} collective-permute-done((bf16[640,640]{1,0:T(8,128)(2,1)S(1)}, bf16[640,640]{1,0:T(8,128)(2,1)S(1)}, u32[]{:S(2)}, u32[]{:S(2)}) %collective-permute-start.3) | collective-permute-done | bytes 819232 | tf_op jit(solution)/shard_map/ppermute | solution.py:341
  58.3 2.5 %collective-permute-start.7 = (bf16[640,640]{1,0:T(8,128)(2,1)}, bf16[640,640]{1,0:T(8,128)(2,1)}, u32[]{:S(2)}, u32[]{:S(2)}) collective-permute-start(bf16[640,640]{1,0:T(8,128)(2,1)} %get-tuple-element.35), channel_id=1, source_target_pairs={{0,8},{4,12},{8,0},{12,4},{16,24},{20,28},{24,16},{28,20},{1,9},{5... | collective-permute-start | bytes 2457608 | tf_op jit(solution)/shard_map/ppermute | solution.py:327
  68.0 11.9 %collective-permute-done.7 = bf16[640,640]{1,0:T(8,128)(2,1)} collective-permute-done((bf16[640,640]{1,0:T(8,128)(2,1)}, bf16[640,640]{1,0:T(8,128)(2,1)}, u32[]{:S(2)}, u32[]{:S(2)}) %collective-permute-start.7) | collective-permute-done | bytes 819232 | tf_op jit(solution)/shard_map/ppermute | solution.py:327
  87.4 3.5 %collective-permute-done.9 = bf16[512,640]{1,0:T(8,128)(2,1)S(1)} collective-permute-done((bf16[512,640]{1,0:T(8,128)(2,1)S(1)}, bf16[512,640]{1,0:T(8,128)(2,1)S(1)}, u32[]{:S(2)}, u32[]{:S(2)}) %collective-permute-start.9) | collective-permute-done | bytes 655392 | tf_op jit(solution)/shard_map/ppermute | solution.py:327
  91.0 12.9 %collective-permute-done.10 = bf16[640,640]{1,0:T(8,128)(2,1)S(1)} collective-permute-done((bf16[640,640]{1,0:T(8,128)(2,1)S(1)}, bf16[640,640]{1,0:T(8,128)(2,1)S(1)}, u32[]{:S(2)}, u32[]{:S(2)}) %collective-permute-start.10) | collective-permute-done | bytes 819232 | tf_op jit(solution)/shard_map/ppermute | solution.py:327
  106.1 7.7 %shard_map.92 = bf16[640,640]{1,0:T(8,128)(2,1)S(1)} custom-call(s32[1]{0:T(128)} %bitcast.9.active_ref, f32[640,640]{1,0:T(8,128)S(1)} %convert_add_fusion.grad_ref, bf16[640,640]{1,0:T(8,128)(2,1)S(1)} %bitcast_select_fusion.init_ref), custom_call_target="tpu_custom_call" | custom-call | flops 4718592000 | bytes 3276800 | tf_op jit(solution)/shard_map/pallas_call | solution.py:178
  115.8 9.4 %collective-permute-done.11 = bf16[320,640]{1,0:T(8,128)(2,1)S(1)} collective-permute-done((bf16[320,640]{1,0:T(8,128)(2,1)S(1)}, bf16[320,640]{1,0:T(8,128)(2,1)S(1)}, u32[]{:S(2)}, u32[]{:S(2)}) %collective-permute-start.11) | collective-permute-done | bytes 409632 | tf_op jit(solution)/shard_map/ppermute | solution.py:327
  125.3 5.3 %collective-permute-start.12 = (bf16[320,640]{1,0:T(8,128)(2,1)S(1)}, bf16[320,640]{1,0:T(8,128)(2,1)S(1)}, u32[]{:S(2)}, u32[]{:S(2)}) collective-permute-start(bf16[320,640]{1,0:T(8,128)(2,1)S(1)} %get-tuple-element.68), channel_id=1, source_target_pairs={{0,16},{4,20},{24,8},{28,12},{1,17},{5,21},{25,9},{29,13},{2,18},{... | collective-permute-start | bytes 1228808 | tf_op jit(solution)/shard_map/ppermute | solution.py:327
  134.3 3.5 %collective-permute-done.12 = bf16[320,640]{1,0:T(8,128)(2,1)S(1)} collective-permute-done((bf16[320,640]{1,0:T(8,128)(2,1)S(1)}, bf16[320,640]{1,0:T(8,128)(2,1)S(1)}, u32[]{:S(2)}, u32[]{:S(2)}) %collective-permute-start.12) | collective-permute-done | bytes 409632 | tf_op jit(solution)/shard_map/ppermute | solution.py:327
  139.4 7.6 %shard_map.93.att_ref = f32[1024,640]{1,0:T(8,128)S(1)} custom-call(s32[1]{0:T(128)} %bitcast.12.first_ref, bf16[1024,640]{1,0:T(8,128)(2,1)S(1)} %pad_maximum_fusion.q_ref, bf16[512,640]{1,0:T(8,128)(2,1)S(1)} %collective-permute-done.5.kp_ref, bf16[1024,640]{1,0:T(8,128)(2,1)S(1)} %pad_maximum_fusion.1.k_ref, ...), custom_call_target="tpu_custom_call" | custom-call | flops 1677721600 | bytes 7864320 | tf_op jit(solution)/shard_map/pallas_call | solution.py:124
  148.3 5.0 %shard_map.94 = (bf16[512,640]{1,0:T(8,128)(2,1)S(1)}, bf16[512,640]{1,0:T(8,128)(2,1)S(1)}) custom-call(s32[2]{0:T(128)S(1)} %pad_add_fusion.1.which_ref, bf16[1024,640]{1,0:T(8,128)(2,1)S(1)} %pad_maximum_fusion.q_ref, bf16[640,640]{1,0:T(8,128)(2,1)S(1)} %get-tuple-element.58.gate_ref, bf16[640,640]{1,0:T(8,128)(2,1)S(1)} %get-tuple-element.57.lift_ref, ...), custom_call_target="tpu_custom_call" | custom-call | flops 2516582400 | bytes 9011200 | tf_op jit(solution)/shard_map/pallas_call | solution.py:214
  156.5 7.5 %collective-permute-done.19.refs_1_ = bf16[512,640]{1,0:T(8,128)(2,1)S(1)} collective-permute-done((bf16[512,640]{1,0:T(8,128)(2,1)S(1)}, bf16[512,640]{1,0:T(8,128)(2,1)S(1)}, u32[]{:S(2)}, u32[]{:S(2)}) %collective-permute-start.19) | collective-permute-done | bytes 655392 | tf_op jit(solution)/shard_map/ppermute | solution.py:324
  165.5 6.7 %collective-permute-done.21.refs_2_ = bf16[512,640]{1,0:T(8,128)(2,1)S(1)} collective-permute-done((bf16[512,640]{1,0:T(8,128)(2,1)S(1)}, bf16[512,640]{1,0:T(8,128)(2,1)S(1)}, u32[]{:S(2)}, u32[]{:S(2)}) %collective-permute-start.21) | collective-permute-done | bytes 655392 | tf_op jit(solution)/shard_map/ppermute | solution.py:481
  172.2 4.9 %shard_map.95.refs_1_ = f32[512,1280]{1,0:T(8,128)S(1)} custom-call(s32[3]{0:T(128)S(1)} %pad_add_fusion.spot_ref, bf16[5120,1280]{1,0:T(8,128)(2,1)S(1)} %bitcast.36, bf16[512,640]{1,0:T(8,128)(2,1)S(1)} %get-tuple-element.49.refs_0_, bf16[512,640]{1,0:T(8,128)(2,1)S(1)} %collective-permute-done.19.refs_1_, bf16[512,640]{1,0:T(8,128)(2,1)S(1)} %collective-permute-done.21.refs_2_), custom_call_target="tpu_custom_call" | custom-call | flops 20132659200 | bytes 12124160 | tf_op jit(solution)/shard_map/pallas_call | solution.py:270
  180.2 2.7 %shard_map.96.refs_4_ = f32[512,1280]{1,0:T(8,128)S(1)} custom-call(s32[3]{0:T(128)S(1)} %pad_add_fusion.spot_ref, bf16[5120,1280]{1,0:T(8,128)(2,1)S(1)} %bitcast.36, bf16[512,640]{1,0:T(8,128)(2,1)S(1)} %collective-permute-done.20.refs_0_, f32[512,1280]{1,0:T(8,128)S(1)} %shard_map.95.refs_1_), custom_call_target="tpu_custom_call" | custom-call | flops 6710886400 | bytes 7536640 | tf_op jit(solution)/shard_map/pallas_call | solution.py:270
  184.1 6.9 %shard_map.97 = bf16[512,1280]{1,0:T(8,128)(2,1)} custom-call(s32[3]{0:T(128)S(1)} %pad_add_fusion.spot_ref, bf16[5120,1280]{1,0:T(8,128)(2,1)S(1)} %bitcast.36, bf16[512,640]{1,0:T(8,128)(2,1)S(1)} %collective-permute-done.22.refs_0_, bf16[512,640]{1,0:T(8,128)(2,1)S(1)} %collective-permute-done.23.refs_1_, ...), custom_call_target="tpu_custom_call" | custom-call | flops 26843545600 | bytes 14417920 | tf_op jit(solution)/shard_map/pallas_call | solution.py:270
  (127 shorter events, 58.7 us)
Async XLA Ops:
  2.2 18.8 %collective-permute-start = (bf16[512,640]{1,0:T(8,128)(2,1)}, bf16[512,640]{1,0:T(8,128)(2,1)}, u32[]{:S(2)}, u32[]{:S(2)}) collective-permute-start(bf16[512,640]{1,0:T(8,128)(2,1)} %constant_dynamic-slice_fusion.2), channel_id=1, source_target_pairs={{0,4},{4,0},{8,12},{12,8},{16,20},{20,16},{24,28},{28,24},{1,5},{5... | collective-permute-start | bytes 1966088 | tf_op jit(solution)/shard_map/ppermute | solution.py:324
  5.1 29.1 %collective-permute-start.1 = (f32[512]{0:T(512)S(1)}, f32[512]{0:T(512)S(1)}, u32[]{:S(2)}, u32[]{:S(2)}) collective-permute-start(f32[512]{0:T(512)S(1)} %bitcast.39), channel_id=1, source_target_pairs={{0,4},{4,0},{8,12},{12,8},{16,20},{20,16},{24,28},{28,24},{1,5},{5... | collective-permute-start | bytes 6152 | tf_op jit(solution)/shard_map/ppermute | solution.py:324
  7.5 26.8 %collective-permute-start.2 = (bf16[512,640]{1,0:T(8,128)(2,1)}, bf16[512,640]{1,0:T(8,128)(2,1)}, u32[]{:S(2)}, u32[]{:S(2)}) collective-permute-start(bf16[512,640]{1,0:T(8,128)(2,1)} %get-tuple-element.65), channel_id=1, source_target_pairs={{0,4},{4,0},{8,12},{12,8},{16,20},{20,16},{24,28},{28,24},{1,5},{5... | collective-permute-start | bytes 1966088 | tf_op jit(solution)/shard_map/ppermute | solution.py:324
  23.2 16.8 %collective-permute-start.5 = (bf16[512,640]{1,0:T(8,128)(2,1)S(1)}, bf16[512,640]{1,0:T(8,128)(2,1)S(1)}, u32[]{:S(2)}, u32[]{:S(2)}) collective-permute-start(bf16[512,640]{1,0:T(8,128)(2,1)S(1)} %get-tuple-element.60), channel_id=1, source_target_pairs={{0,8},{4,12},{8,16},{12,20},{16,24},{20,28},{1,9},{5,13},{9,17},{1... | collective-permute-start | bytes 1966088 | tf_op jit(solution)/shard_map/ppermute | solution.py:327
  36.2 20.5 %collective-permute-start.3 = (bf16[640,640]{1,0:T(8,128)(2,1)S(1)}, bf16[640,640]{1,0:T(8,128)(2,1)S(1)}, u32[]{:S(2)}, u32[]{:S(2)}) collective-permute-start(bf16[640,640]{1,0:T(8,128)(2,1)S(1)} %get-tuple-element.73), channel_id=1, source_target_pairs={{0,8},{4,12},{24,16},{28,20},{25,17},{29,21},{1,9},{5,13},{2,10},{... | collective-permute-start | bytes 2457608 | tf_op jit(solution)/shard_map/ppermute | solution.py:341
  42.9 15.4 %collective-permute-start.6 = (bf16[512,640]{1,0:T(8,128)(2,1)S(1)}, bf16[512,640]{1,0:T(8,128)(2,1)S(1)}, u32[]{:S(2)}, u32[]{:S(2)}) collective-permute-start(bf16[512,640]{1,0:T(8,128)(2,1)S(1)} %get-tuple-element.36), channel_id=1, source_target_pairs={{8,16},{12,20},{16,24},{20,28},{9,17},{13,21},{17,25},{21,29},{10,... | collective-permute-start | bytes 1966088 | tf_op jit(solution)/shard_map/ppermute | solution.py:327
  58.3 21.6 %collective-permute-start.7 = (bf16[640,640]{1,0:T(8,128)(2,1)}, bf16[640,640]{1,0:T(8,128)(2,1)}, u32[]{:S(2)}, u32[]{:S(2)}) collective-permute-start(bf16[640,640]{1,0:T(8,128)(2,1)} %get-tuple-element.35), channel_id=1, source_target_pairs={{0,8},{4,12},{8,0},{12,4},{16,24},{20,28},{24,16},{28,20},{1,9},{5... | collective-permute-start | bytes 2457608 | tf_op jit(solution)/shard_map/ppermute | solution.py:327
  61.7 24.3 %collective-permute-start.8 = (bf16[640,640]{1,0:T(8,128)(2,1)}, bf16[640,640]{1,0:T(8,128)(2,1)}, u32[]{:S(2)}, u32[]{:S(2)}) collective-permute-start(bf16[640,640]{1,0:T(8,128)(2,1)} %get-tuple-element.55), channel_id=1, source_target_pairs={{16,8},{20,12},{9,17},{13,21},{18,10},{22,14},{11,19},{15,23}} | collective-permute-start | bytes 2457608 | tf_op jit(solution)/shard_map/ppermute | solution.py:341
  66.2 24.8 %collective-permute-start.9 = (bf16[512,640]{1,0:T(8,128)(2,1)S(1)}, bf16[512,640]{1,0:T(8,128)(2,1)S(1)}, u32[]{:S(2)}, u32[]{:S(2)}) collective-permute-start(bf16[512,640]{1,0:T(8,128)(2,1)S(1)} %copy-done.9), channel_id=1, source_target_pairs={{0,8},{4,12},{1,9},{5,13},{2,10},{6,14},{3,11},{7,15}} | collective-permute-start | bytes 1966088 | tf_op jit(solution)/shard_map/ppermute | solution.py:327
  82.0 22.0 %collective-permute-start.10 = (bf16[640,640]{1,0:T(8,128)(2,1)S(1)}, bf16[640,640]{1,0:T(8,128)(2,1)S(1)}, u32[]{:S(2)}, u32[]{:S(2)}) collective-permute-start(bf16[640,640]{1,0:T(8,128)(2,1)S(1)} %get-tuple-element.53), channel_id=1, source_target_pairs={{16,0},{20,4},{8,24},{12,28},{17,1},{21,5},{9,25},{13,29},{18,2},{... | collective-permute-start | bytes 2457608 | tf_op jit(solution)/shard_map/ppermute | solution.py:327
  84.5 30.9 %collective-permute-start.4 = (bf16[512,640]{1,0:T(8,128)(2,1)S(1)}, bf16[512,640]{1,0:T(8,128)(2,1)S(1)}, u32[]{:S(2)}, u32[]{:S(2)}) collective-permute-start(bf16[512,640]{1,0:T(8,128)(2,1)S(1)} %copy-done.18), channel_id=1, source_target_pairs={{0,4},{4,0},{8,12},{12,8},{16,20},{20,16},{24,28},{28,24},{1,5},{5... | collective-permute-start | bytes 1966088 | tf_op jit(solution)/shard_map/ppermute | solution.py:324
  104.1 29.3 %collective-permute-start.17 = (bf16[640,640]{1,0:T(8,128)(2,1)S(1)}, bf16[640,640]{1,0:T(8,128)(2,1)S(1)}, u32[]{:S(2)}, u32[]{:S(2)}) collective-permute-start(bf16[640,640]{1,0:T(8,128)(2,1)S(1)} %shard_map.91), channel_id=1, source_target_pairs={{8,16},{12,20},{17,9},{21,13},{10,18},{14,22},{19,11},{23,15}} | collective-permute-start | bytes 2457608 | tf_op jit(solution)/shard_map/ppermute | solution.py:341
  104.8 28.6 %collective-permute-start.16 = (bf16[640,640]{1,0:T(8,128)(2,1)S(1)}, bf16[640,640]{1,0:T(8,128)(2,1)S(1)}, u32[]{:S(2)}, u32[]{:S(2)}) collective-permute-start(bf16[640,640]{1,0:T(8,128)(2,1)S(1)} %shard_map.91), channel_id=1, source_target_pairs={{8,0},{12,4},{17,25},{21,29},{10,2},{14,6},{19,27},{23,31}} | collective-permute-start | bytes 2457608 | tf_op jit(solution)/shard_map/ppermute | solution.py:341
  113.9 11.3 %collective-permute-start.11 = (bf16[320,640]{1,0:T(8,128)(2,1)S(1)}, bf16[320,640]{1,0:T(8,128)(2,1)S(1)}, u32[]{:S(2)}, u32[]{:S(2)}) collective-permute-start(bf16[320,640]{1,0:T(8,128)(2,1)S(1)} %slice.8), channel_id=1, source_target_pairs={{0,16},{4,20},{24,8},{28,12},{1,17},{5,21},{25,9},{29,13},{2,18},{... | collective-permute-start | bytes 1228808 | tf_op jit(solution)/shard_map/ppermute | solution.py:327
  125.3 12.5 %collective-permute-start.12 = (bf16[320,640]{1,0:T(8,128)(2,1)S(1)}, bf16[320,640]{1,0:T(8,128)(2,1)S(1)}, u32[]{:S(2)}, u32[]{:S(2)}) collective-permute-start(bf16[320,640]{1,0:T(8,128)(2,1)S(1)} %get-tuple-element.68), channel_id=1, source_target_pairs={{0,16},{4,20},{24,8},{28,12},{1,17},{5,21},{25,9},{29,13},{2,18},{... | collective-permute-start | bytes 1228808 | tf_op jit(solution)/shard_map/ppermute | solution.py:327
  130.7 17.1 %collective-permute-start.13 = (bf16[640,640]{1,0:T(8,128)(2,1)S(1)}, bf16[640,640]{1,0:T(8,128)(2,1)S(1)}, u32[]{:S(2)}, u32[]{:S(2)}) collective-permute-start(bf16[640,640]{1,0:T(8,128)(2,1)S(1)} %shard_map.92), channel_id=1, source_target_pairs={{0,8},{4,12},{24,16},{28,20},{1,9},{5,13},{25,17},{29,21},{2,10},{... | collective-permute-start | bytes 2457608 | tf_op jit(solution)/shard_map/ppermute | solution.py:327
  132.1 15.0 %collective-permute-start.14 = (bf16[320,640]{1,0:T(8,128)(2,1)S(1)}, bf16[320,640]{1,0:T(8,128)(2,1)S(1)}, u32[]{:S(2)}, u32[]{:S(2)}) collective-permute-start(bf16[320,640]{1,0:T(8,128)(2,1)S(1)} %collective-permute-done.11), channel_id=1, source_target_pairs={{8,0},{12,4},{16,24},{20,28},{9,1},{13,5},{17,25},{21,29},{10,2},{... | collective-permute-start | bytes 1228808 | tf_op jit(solution)/shard_map/ppermute | solution.py:327
  133.5 14.7 %collective-permute-start.18 = (bf16[640,640]{1,0:T(8,128)(2,1)S(1)}, bf16[640,640]{1,0:T(8,128)(2,1)S(1)}, u32[]{:S(2)}, u32[]{:S(2)}) collective-permute-start(bf16[640,640]{1,0:T(8,128)(2,1)S(1)} %select_select_fusion), channel_id=1, source_target_pairs={{16,24},{20,28},{9,1},{13,5},{18,26},{22,30},{11,3},{15,7}} | collective-permute-start | bytes 2457608 | tf_op jit(solution)/shard_map/ppermute | solution.py:341
  137.8 10.0 %collective-permute-start.15 = (bf16[320,640]{1,0:T(8,128)(2,1)S(1)}, bf16[320,640]{1,0:T(8,128)(2,1)S(1)}, u32[]{:S(2)}, u32[]{:S(2)}) collective-permute-start(bf16[320,640]{1,0:T(8,128)(2,1)S(1)} %collective-permute-done.12), channel_id=1, source_target_pairs={{8,0},{12,4},{16,24},{20,28},{9,1},{13,5},{17,25},{21,29},{10,2},{... | collective-permute-start | bytes 1228808 | tf_op jit(solution)/shard_map/ppermute | solution.py:327
  153.3 10.7 %collective-permute-start.19 = (bf16[512,640]{1,0:T(8,128)(2,1)S(1)}, bf16[512,640]{1,0:T(8,128)(2,1)S(1)}, u32[]{:S(2)}, u32[]{:S(2)}) collective-permute-start(bf16[512,640]{1,0:T(8,128)(2,1)S(1)} %get-tuple-element.47), channel_id=1, source_target_pairs={{0,4},{4,0},{8,12},{12,8},{16,20},{20,16},{24,28},{28,24},{1,5},{5... | collective-permute-start | bytes 1966088 | tf_op jit(solution)/shard_map/ppermute | solution.py:324
  154.9 17.2 %collective-permute-start.21 = (bf16[512,640]{1,0:T(8,128)(2,1)S(1)}, bf16[512,640]{1,0:T(8,128)(2,1)S(1)}, u32[]{:S(2)}, u32[]{:S(2)}) collective-permute-start(bf16[512,640]{1,0:T(8,128)(2,1)S(1)} %get-tuple-element.49.refs_0_), channel_id=1, source_target_pairs={{0,2},{1,3},{2,0},{3,1},{4,6},{5,7},{6,4},{7,5},{8,10},{9,11},{10,... | collective-permute-start | bytes 1966088 | tf_op jit(solution)/shard_map/ppermute | solution.py:481
  164.0 15.2 %collective-permute-start.20 = (bf16[512,640]{1,0:T(8,128)(2,1)S(1)}, bf16[512,640]{1,0:T(8,128)(2,1)S(1)}, u32[]{:S(2)}, u32[]{:S(2)}) collective-permute-start(bf16[512,640]{1,0:T(8,128)(2,1)S(1)} %collective-permute-done.19.refs_1_), channel_id=1, source_target_pairs={{0,2},{1,3},{2,0},{3,1},{4,6},{5,7},{6,4},{7,5},{8,10},{9,11},{10,... | collective-permute-start | bytes 1966088 | tf_op jit(solution)/shard_map/ppermute | solution.py:481
  179.2 3.7 %collective-permute-start.23 = (bf16[512,640]{1,0:T(8,128)(2,1)S(1)}, bf16[512,640]{1,0:T(8,128)(2,1)S(1)}, u32[]{:S(2)}, u32[]{:S(2)}) collective-permute-start(bf16[512,640]{1,0:T(8,128)(2,1)S(1)} %collective-permute-done.19.refs_1_), channel_id=1, source_target_pairs={{0,1},{1,0},{2,3},{3,2},{4,5},{5,4},{6,7},{7,6},{8,9},{9,8},{10,11... | collective-permute-start | bytes 1966088 | tf_op jit(solution)/shard_map/ppermute | solution.py:481
  179.7 4.4 %collective-permute-start.25 = (bf16[512,640]{1,0:T(8,128)(2,1)S(1)}, bf16[512,640]{1,0:T(8,128)(2,1)S(1)}, u32[]{:S(2)}, u32[]{:S(2)}) collective-permute-start(bf16[512,640]{1,0:T(8,128)(2,1)S(1)} %collective-permute-done.20.refs_0_), channel_id=1, source_target_pairs={{0,1},{1,0},{2,3},{3,2},{4,5},{5,4},{6,7},{7,6},{8,9},{9,8},{10,11... | collective-permute-start | bytes 1966088 | tf_op jit(solution)/shard_map/ppermute | solution.py:481
  (27 other events, 230.9 us)
where the time goes:
time: 192 us; the launch traced here: 191 us
  waiting for transfers between devices  73.9 us (38%)
  starting transfers between devices  41.8 us (22%)
  Pallas kernels  34.9 us (18%)
  matrix products  17.2 us (9%)
  other arithmetic  13.9 us (7%)
  local copies, waits for them, and re-layouts  8.71 us (5%)
    ppermute x10, waiting for transfers between devices, between_planes(): lax.ppermute(array, 'ctx', [(a * group + m, b * group + m) for a, b in pa...  41.9 us
    ppermute x10, starting transfers between devices, between_planes(): lax.ppermute(array, 'ctx', [(a * group + m, b * group + m) for a, b in pa...  21.5 us
    dot_general x12, matrix products, mm(): return lax.dot_general(a, b, (dims, ((), ())), preferred_element_type=f32)  17.2 us
    ppermute x5, waiting for transfers between devices, to_member(): return lax.ppermute(array, 'ctx', pairs)  14.8 us
    pallas_call x3, Pallas kernels, project(): pl.pallas_call(functools.partial(project_kernel, origins, group, total is...  14.5 us
    ppermute x6, waiting for transfers between devices, swapped(): return lax.ppermute(part, 'head', [(i, i ^ bit) for i in range(columns_of)])  9.95 us
    ppermute x5, starting transfers between devices, to_member(): return lax.ppermute(array, 'ctx', pairs)  8.16 us
    ppermute x5, starting transfers between devices, by_side(): return lax.ppermute(array, ('ctx', 'head'), moves)  8.16 us
  transfers between devices with their start and end apart: 26, of which 14 were waited for; matrix products, arithmetic and copies ran while one was open for 18% of the time, Pallas kernels for 12%

commit v1 on v0

--- a/solution.py
+++ b/solution.py
@@ -13,7 +13,6 @@
 NS_ITERS = 3
 PIECES = 2
 VMEM_BYTES = 20 * 1024 * 1024
-PROJECT_BYTES = 28 * 1024 * 1024
 
 quintic_first = 3.4445
 quintic_second = -4.775
@@ -229,59 +228,73 @@
     )(jnp.stack(order).astype(jnp.int32), q, gate, lift, down, attended, gain)
 
 
-def project_kernel(origins, group, has_total, spot_ref, w_ref, *refs):
-    count = len(origins)
+def fetch_kernel(groups, group, depth, spot_ref, w_ref, after_ref, *refs):
+    arrived = refs[-1]
+    copies = []
+    for origins, out_ref in zip(groups, refs[:-1]):
+        for number, (offset, head) in enumerate(origins):
+            start = ((spot_ref[0] ^ offset) * group + spot_ref[1 + head]) * depth
+            copy = pltpu.make_async_copy(
+                w_ref.at[pl.ds(pl.multiple_of(start, depth), depth)],
+                out_ref.at[pl.ds(number * depth, depth)],
+                arrived.at[len(copies)],
+            )
+            copy.start()
+            copies.append(copy)
+    for copy in copies:
+        copy.wait()
+
+
+def fetched(groups, group, depth, spot, weight, after_this):
+    columns, count = weight.shape[1], sum(map(len, groups))
+    hbm = pl.BlockSpec(memory_space=pltpu.HBM)
+    return pl.pallas_call(
+        functools.partial(fetch_kernel, groups, group, depth),
+        out_shape=[jax.ShapeDtypeStruct((len(g) * depth, columns), bf16) for g in groups],
+        in_specs=[pl.BlockSpec(memory_space=pltpu.SMEM), hbm, hbm],
+        out_specs=[pl.BlockSpec(memory_space=pltpu.VMEM)] * len(groups),
+        scratch_shapes=[pltpu.SemaphoreType.DMA((count,))],
+        compiler_params=pltpu.CompilerParams(vmem_limit_bytes=VMEM_BYTES),
+        cost_estimate=pl.CostEstimate(
+            flops=10**10, bytes_accessed=4 * count * depth * columns, transcendentals=0
+        ),
+    )(spot, weight, after_this)
+
+
+def project_kernel(count, rows_ref, *refs):
     chunk_refs = refs[:count]
-    total_ref = refs[count] if has_total else None
-    out_ref, joined, w_rows, arrived = refs[-4:]
+    total_ref = refs[count] if len(refs) == count + 3 else None
+    out_ref, joined = refs[-2:]
     depth = chunk_refs[0].shape[1]
-    copies = []
-    for number, (offset, head) in enumerate(origins):
-        start = ((spot_ref[0] ^ offset) * group + spot_ref[1 + head]) * depth
-        copy = pltpu.make_async_copy(
-            w_ref.at[pl.ds(pl.multiple_of(start, depth), depth)],
-            w_rows.at[pl.ds(number * depth, depth)],
-            arrived.at[number],
-        )
-        copy.start()
-        copies.append(copy)
     for number in range(count):
         joined[:, number * depth : (number + 1) * depth] = chunk_refs[number][...]
-    for copy in copies:
-        copy.wait()
     tile = math.gcd(out_ref.shape[1], 256)
 
     @pl.loop(0, out_ref.shape[1] // tile)
     def _(number):
         at = pl.ds(pl.multiple_of(number * tile, tile), tile)
-        result = mm(joined[...], w_rows[:, at])
-        if has_total:
+        result = mm(joined[...], rows_ref[:, at])
+        if total_ref is not None:
             result += total_ref[:, at]
         out_ref[:, at] = result.astype(out_ref.dtype)
 
 
-def project(parts, group, spot, weight, total, is_last):
-    chunks, origins = [part[0] for part in parts], [part[1:] for part in parts]
+def project(chunks, rows, total, is_last):
     count = len(chunks)
-    rows, depth = chunks[0].shape
-    columns = weight.shape[1]
+    tokens, depth = chunks[0].shape
+    columns = rows.shape[1]
     vmem = pl.BlockSpec(memory_space=pltpu.VMEM)
-    operands = [spot, weight] + list(chunks) + ([] if total is None else [total])
+    operands = [rows] + list(chunks) + ([] if total is None else [total])
     return pl.pallas_call(
-        functools.partial(project_kernel, origins, group, total is not None),
-        out_shape=jax.ShapeDtypeStruct((rows, columns), bf16 if is_last else f32),
-        in_specs=[pl.BlockSpec(memory_space=pltpu.SMEM), pl.BlockSpec(memory_space=pltpu.HBM)]
-        + [vmem] * (len(operands) - 2),
+        functools.partial(project_kernel, count),
+        out_shape=jax.ShapeDtypeStruct((tokens, columns), bf16 if is_last else f32),
+        in_specs=[vmem] * len(operands),
         out_specs=vmem,
-        scratch_shapes=[
-            pltpu.VMEM((rows, count * depth), bf16),
-            pltpu.VMEM((count * depth, columns), bf16),
-            pltpu.SemaphoreType.DMA((count,)),
-        ],
-        compiler_params=pltpu.CompilerParams(vmem_limit_bytes=PROJECT_BYTES),
+        scratch_shapes=[pltpu.VMEM((tokens, count * depth), bf16)],
+        compiler_params=pltpu.CompilerParams(vmem_limit_bytes=VMEM_BYTES),
         cost_estimate=pl.CostEstimate(
-            flops=16 * count * rows * depth * columns,
-            bytes_accessed=2 * count * (rows + columns) * depth + 8 * rows * columns,
+            flops=16 * count * tokens * depth * columns,
+            bytes_accessed=2 * count * depth * (tokens + columns),
             transcendentals=0,
         ),
     )(*operands)
@@ -493,14 +506,20 @@
     spot = jnp.stack([head_place] + [head for _, head in arrived]).astype(jnp.int32)
     parts = [(chunk, 0, number) for number, (chunk, _) in enumerate(arrived)]
     parts += [(swapped(chunk, bits[0]), bits[0], number) for number, (chunk, _) in enumerate(arrived)]
-    total = project(parts[:-1], group, spot, output_weight, None, False)
-    last, offset, number = parts[-1]
-    parts[-1] = (after(last, total), offset, number)
-    copies = [(after(part, parts[-1][0]), o, n) for part, o, n in parts]
+    places = [part[1:] for part in parts]
+    found = list(places)
     for bit in bits[1:]:
-        copies += [(swapped(part, bit), o ^ bit, n) for part, o, n in copies]
-    total = project(parts[-1:], group, spot, output_weight, total, False)
-    return project(copies[len(parts) :], group, spot, output_weight, total, True)
+        found += [(o ^ bit, n) for o, n in found]
+    groups = [places[:-1], places[-1:], found[len(places) :]]
+    rows = fetched(groups, group, width, spot, output_weight, combined)
+    chunks = [part[0] for part in parts]
+    total = project(chunks[:-1], rows[0], None, False)
+    chunks[-1] = after(chunks[-1], total)
+    copies = [after(chunk, total) for chunk in chunks]
+    for bit in bits[1:]:
+        copies += [swapped(chunk, bit) for chunk in copies]
+    total = project(chunks[-1:], rows[1], total, False)
+    return project(copies[len(chunks) :], rows[2], total, True)
 
 
 def solution(mesh):

time: 192 us -> 189 us (0.984)
  waiting for transfers between devices: 73.9 us -> 70.2 us
  local copies, waits for them, and re-layouts: 8.71 us -> 10.7 us
    ppermute x5, waiting for transfers between devices: 14.8 us -> 12.6 us  [to_member(): return lax.ppermute(array, 'ctx', pairs)]
    pallas_call x3 -> x4, Pallas kernels: 14.5 us -> 13.4 us  [the longest x3 11.2 us: project(): pl.pallas_call(functools.partial(project_kernel, count), out_shape=jax.Sh...]
    unnamed x50 -> x48, local copies, waits for them, and re-layouts: 3.24 us -> 4.1 us
  transfers between devices with their start and end apart: 26 -> 26, of which waited for: 14 -> 13; matrix products, arithmetic and copies ran while one was open for 18% -> 19% of each run, Pallas kernels for 12% -> 12%
where the time goes in v1:
time: 189 us; the launch traced here: 188 us
  waiting for transfers between devices  70.2 us (37%)
  starting transfers between devices  41.2 us (22%)
  Pallas kernels  33.8 us (18%)
  matrix products  17.2 us (9%)
  other arithmetic  14 us (7%)
  local copies, waits for them, and re-layouts  10.7 us (6%)
    ppermute x10, waiting for transfers between devices, between_planes(): lax.ppermute(array, 'ctx', [(a * group + m, b * group + m) for a, b in pa...  40.9 us
    ppermute x10, starting transfers between devices, between_planes(): lax.ppermute(array, 'ctx', [(a * group + m, b * group + m) for a, b in pa...  21.3 us
    dot_general x12, matrix products, mm(): return lax.dot_general(a, b, (dims, ((), ())), preferred_element_type=f32)  17.2 us
    ppermute x5, waiting for transfers between devices, to_member(): return lax.ppermute(array, 'ctx', pairs)  12.6 us
    pallas_call x3, Pallas kernels, project(): pl.pallas_call(functools.partial(project_kernel, count), out_shape=jax.Sh...  11.2 us
    ppermute x6, waiting for transfers between devices, swapped(): return lax.ppermute(part, 'head', [(i, i ^ bit) for i in range(columns_of)])  9.5 us
    ppermute x5, starting transfers between devices, by_side(): return lax.ppermute(array, ('ctx', 'head'), moves)  8.2 us
    ppermute x5, starting transfers between devices, to_member(): return lax.ppermute(array, 'ctx', pairs)  8.17 us
  transfers between devices with their start and end apart: 26, of which 13 were waited for; matrix products, arithmetic and copies ran while one was open for 19% of the time, Pallas kernels for 12%

profile of v1, /device:TPU:0, one launch (start us, length us, event | category | flops | bytes accessed | tf_op | source)
XLA Modules:
  0.0 187.8 jit_solution(16081976915390011160)
XLA Ops:
  2.2 3.0 %collective-permute-start = (bf16[512,640]{1,0:T(8,128)(2,1)}, bf16[512,640]{1,0:T(8,128)(2,1)}, u32[]{:S(2)}, u32[]{:S(2)}) collective-permute-start(bf16[512,640]{1,0:T(8,128)(2,1)} %constant_dynamic-slice_fusion.2), channel_id=1, source_target_pairs={{0,4},{4,0},{8,12},{12,8},{16,20},{20,16},{24,28},{28,24},{1,5},{5... | collective-permute-start | bytes 1966088 | tf_op jit(solution)/shard_map/ppermute | solution.py:337
  5.2 2.2 %constant_dynamic-slice_fusion = (bf16[512,640]{1,0:T(8,128)(2,1)}, bf16[512,640]{1,0:T(8,128)(2,1)S(1)}) fusion(bf16[512,1280]{1,0:T(8,128)(2,1)} %param.11, s32[]{:T(128)S(6)} %select_n.197, s32[]{:T(128)S(6)} %select_n.198), kind=kLoop, calls=%fused_computation.65 | loop fusion | bytes 2621448 | tf_op jit(solution)/shard_map/dynamic_slice | solution.py:357
  17.0 4.0 %collective-permute-done = bf16[512,640]{1,0:T(8,128)(2,1)} collective-permute-done((bf16[512,640]{1,0:T(8,128)(2,1)}, bf16[512,640]{1,0:T(8,128)(2,1)}, u32[]{:S(2)}, u32[]{:S(2)}) %collective-permute-start) | collective-permute-done | bytes 655392 | tf_op jit(solution)/shard_map/ppermute | solution.py:337
  23.2 4.1 %collective-permute-start.5 = (bf16[512,640]{1,0:T(8,128)(2,1)S(1)}, bf16[512,640]{1,0:T(8,128)(2,1)S(1)}, u32[]{:S(2)}, u32[]{:S(2)}) collective-permute-start(bf16[512,640]{1,0:T(8,128)(2,1)S(1)} %get-tuple-element.66), channel_id=1, source_target_pairs={{0,8},{4,12},{8,16},{12,20},{16,24},{20,28},{1,9},{5,13},{9,17},{1... | collective-permute-start | bytes 1966088 | tf_op jit(solution)/shard_map/ppermute | solution.py:340
  31.0 3.3 %collective-permute-done.2 = bf16[512,640]{1,0:T(8,128)(2,1)} collective-permute-done((bf16[512,640]{1,0:T(8,128)(2,1)}, bf16[512,640]{1,0:T(8,128)(2,1)}, u32[]{:S(2)}, u32[]{:S(2)}) %collective-permute-start.2) | collective-permute-done | bytes 655392 | tf_op jit(solution)/shard_map/ppermute | solution.py:337
  36.2 3.8 %collective-permute-start.3 = (bf16[640,640]{1,0:T(8,128)(2,1)S(1)}, bf16[640,640]{1,0:T(8,128)(2,1)S(1)}, u32[]{:S(2)}, u32[]{:S(2)}) collective-permute-start(bf16[640,640]{1,0:T(8,128)(2,1)S(1)} %get-tuple-element.79), channel_id=1, source_target_pairs={{0,8},{4,12},{24,16},{28,20},{25,17},{29,21},{1,9},{5,13},{2,10},{... | collective-permute-start | bytes 2457608 | tf_op jit(solution)/shard_map/ppermute | solution.py:354
  45.6 3.9 %select_convert_fusion = (bf16[640,640]{1,0:T(8,128)(2,1)}, f32[640,640]{1,0:T(8,128)}) fusion(f32[640,640]{1,0:T(8,128)S(1)} %convolution_add_fusion.1, pred[]{:T(512)S(6)} %eq.77, f32[640,640]{1,0:T(8,128)S(1)} %fusion.13, bf16[512,640]{1,0:T(8,128)(2,1)} %collective-permute-done, f32[512,640]{1,0:T(8,128)S(1)} %fusion.40, ...), kind=kOutput, calls=%fused_computation.3 | convolution fusion | flops 423526400 | bytes 10321921 | tf_op jit(solution)/shard_map/dot_general | solution.py:26
  49.5 7.2 %collective-permute-done.3 = bf16[640,640]{1,0:T(8,128)(2,1)S(1)} collective-permute-done((bf16[640,640]{1,0:T(8,128)(2,1)S(1)}, bf16[640,640]{1,0:T(8,128)(2,1)S(1)}, u32[]{:S(2)}, u32[]{:S(2)}) %collective-permute-start.3) | collective-permute-done | bytes 819232 | tf_op jit(solution)/shard_map/ppermute | solution.py:354
  59.2 2.5 %collective-permute-start.7 = (bf16[640,640]{1,0:T(8,128)(2,1)}, bf16[640,640]{1,0:T(8,128)(2,1)}, u32[]{:S(2)}, u32[]{:S(2)}) collective-permute-start(bf16[640,640]{1,0:T(8,128)(2,1)} %get-tuple-element.38), channel_id=1, source_target_pairs={{0,8},{4,12},{8,0},{12,4},{16,24},{20,28},{24,16},{28,20},{1,9},{5... | collective-permute-start | bytes 2457608 | tf_op jit(solution)/shard_map/ppermute | solution.py:340
  69.8 10.8 %collective-permute-done.7 = bf16[640,640]{1,0:T(8,128)(2,1)} collective-permute-done((bf16[640,640]{1,0:T(8,128)(2,1)}, bf16[640,640]{1,0:T(8,128)(2,1)}, u32[]{:S(2)}, u32[]{:S(2)}) %collective-permute-start.7) | collective-permute-done | bytes 819232 | tf_op jit(solution)/shard_map/ppermute | solution.py:340
  88.2 3.5 %collective-permute-done.9 = bf16[512,640]{1,0:T(8,128)(2,1)S(1)} collective-permute-done((bf16[512,640]{1,0:T(8,128)(2,1)S(1)}, bf16[512,640]{1,0:T(8,128)(2,1)S(1)}, u32[]{:S(2)}, u32[]{:S(2)}) %collective-permute-start.9) | collective-permute-done | bytes 655392 | tf_op jit(solution)/shard_map/ppermute | solution.py:340
  91.8 12.9 %collective-permute-done.10 = bf16[640,640]{1,0:T(8,128)(2,1)S(1)} collective-permute-done((bf16[640,640]{1,0:T(8,128)(2,1)S(1)}, bf16[640,640]{1,0:T(8,128)(2,1)S(1)}, u32[]{:S(2)}, u32[]{:S(2)}) %collective-permute-start.10) | collective-permute-done | bytes 819232 | tf_op jit(solution)/shard_map/ppermute | solution.py:340
  106.9 7.7 %shard_map.92 = bf16[640,640]{1,0:T(8,128)(2,1)S(1)} custom-call(s32[1]{0:T(128)} %bitcast.9.active_ref, f32[640,640]{1,0:T(8,128)S(1)} %convert_add_fusion.grad_ref, bf16[640,640]{1,0:T(8,128)(2,1)S(1)} %bitcast_select_fusion.init_ref), custom_call_target="tpu_custom_call" | custom-call | flops 4718592000 | bytes 3276800 | tf_op jit(solution)/shard_map/pallas_call | solution.py:177
  116.6 9.4 %collective-permute-done.11 = bf16[320,640]{1,0:T(8,128)(2,1)S(1)} collective-permute-done((bf16[320,640]{1,0:T(8,128)(2,1)S(1)}, bf16[320,640]{1,0:T(8,128)(2,1)S(1)}, u32[]{:S(2)}, u32[]{:S(2)}) %collective-permute-start.11) | collective-permute-done | bytes 409632 | tf_op jit(solution)/shard_map/ppermute | solution.py:340
  126.0 5.3 %collective-permute-start.12 = (bf16[320,640]{1,0:T(8,128)(2,1)S(1)}, bf16[320,640]{1,0:T(8,128)(2,1)S(1)}, u32[]{:S(2)}, u32[]{:S(2)}) collective-permute-start(bf16[320,640]{1,0:T(8,128)(2,1)S(1)} %get-tuple-element.74), channel_id=1, source_target_pairs={{0,16},{4,20},{24,8},{28,12},{1,17},{5,21},{25,9},{29,13},{2,18},{... | collective-permute-start | bytes 1228808 | tf_op jit(solution)/shard_map/ppermute | solution.py:340
  135.0 3.6 %collective-permute-done.12 = bf16[320,640]{1,0:T(8,128)(2,1)S(1)} collective-permute-done((bf16[320,640]{1,0:T(8,128)(2,1)S(1)}, bf16[320,640]{1,0:T(8,128)(2,1)S(1)}, u32[]{:S(2)}, u32[]{:S(2)}) %collective-permute-start.12) | collective-permute-done | bytes 409632 | tf_op jit(solution)/shard_map/ppermute | solution.py:340
  140.2 7.6 %shard_map.93.att_ref = f32[1024,640]{1,0:T(8,128)S(1)} custom-call(s32[1]{0:T(128)} %bitcast.12.first_ref, bf16[1024,640]{1,0:T(8,128)(2,1)S(1)} %pad_maximum_fusion.q_ref, bf16[512,640]{1,0:T(8,128)(2,1)S(1)} %collective-permute-done.5.kp_ref, bf16[1024,640]{1,0:T(8,128)(2,1)S(1)} %pad_maximum_fusion.1.k_ref, ...), custom_call_target="tpu_custom_call" | custom-call | flops 1677721600 | bytes 7864320 | tf_op jit(solution)/shard_map/pallas_call | solution.py:123
  149.2 5.0 %shard_map.94 = (bf16[512,640]{1,0:T(8,128)(2,1)S(1)}, bf16[512,640]{1,0:T(8,128)(2,1)S(1)}) custom-call(s32[2]{0:T(128)S(1)} %pad_add_fusion.1.which_ref, bf16[1024,640]{1,0:T(8,128)(2,1)S(1)} %pad_maximum_fusion.q_ref, bf16[640,640]{1,0:T(8,128)(2,1)S(1)} %get-tuple-element.64.gate_ref, bf16[640,640]{1,0:T(8,128)(2,1)S(1)} %get-tuple-element.63.lift_ref, ...), custom_call_target="tpu_custom_call" | custom-call | flops 2516582400 | bytes 9011200 | tf_op jit(solution)/shard_map/pallas_call | solution.py:213
  157.3 2.2 %shard_map.95 = (bf16[1920,1280]{1,0:T(8,128)(2,1)S(1)}, bf16[640,1280]{1,0:T(8,128)(2,1)S(1)}, bf16[2560,1280]{1,0:T(8,128)(2,1)S(1)}) custom-call(s32[3]{0:T(128)S(1)} %pad_add_fusion.spot_ref, bf16[5120,1280]{1,0:T(8,128)(2,1)S(1)} %bitcast.36, bf16[512,640]{1,0:T(8,128)(2,1)S(1)} %get-tuple-element.53.after_ref.refs_0_), custom_call_target="tpu_custom_call" | custom-call | flops 10000000000 | bytes 26214400 | tf_op jit(solution)/shard_map/pallas_call | solution.py:251
  159.6 5.3 %collective-permute-done.19.refs_1_ = bf16[512,640]{1,0:T(8,128)(2,1)S(1)} collective-permute-done((bf16[512,640]{1,0:T(8,128)(2,1)S(1)}, bf16[512,640]{1,0:T(8,128)(2,1)S(1)}, u32[]{:S(2)}, u32[]{:S(2)}) %collective-permute-start.19) | collective-permute-done | bytes 655392 | tf_op jit(solution)/shard_map/ppermute | solution.py:337
  166.4 6.7 %collective-permute-done.20.refs_2_ = bf16[512,640]{1,0:T(8,128)(2,1)S(1)} collective-permute-done((bf16[512,640]{1,0:T(8,128)(2,1)S(1)}, bf16[512,640]{1,0:T(8,128)(2,1)S(1)}, u32[]{:S(2)}, u32[]{:S(2)}) %collective-permute-start.20) | collective-permute-done | bytes 655392 | tf_op jit(solution)/shard_map/ppermute | solution.py:494
  173.1 3.7 %shard_map.96.refs_1_ = f32[512,1280]{1,0:T(8,128)S(1)} custom-call(bf16[1920,1280]{1,0:T(8,128)(2,1)S(1)} %get-tuple-element.51.rows_ref, bf16[512,640]{1,0:T(8,128)(2,1)S(1)} %get-tuple-element.53.after_ref.refs_0_, bf16[512,640]{1,0:T(8,128)(2,1)S(1)} %collective-permute-done.19.refs_1_, bf16[512,640]{1,0:T(8,128)(2,1)S(1)} %collective-permute-done.20.refs_2_), custom_call_target="tpu_custom_call" | custom-call | flops 20132659200 | bytes 6881280 | tf_op jit(solution)/shard_map/pallas_call | solution.py:288
  177.5 2.6 %collective-permute-done.24.refs_0_ = bf16[512,640]{1,0:T(8,128)(2,1)S(1)} collective-permute-done((bf16[512,640]{1,0:T(8,128)(2,1)S(1)}, bf16[512,640]{1,0:T(8,128)(2,1)S(1)}, u32[]{:S(2)}, u32[]{:S(2)}) %collective-permute-start.24) | collective-permute-done | bytes 655392 | tf_op jit(solution)/shard_map/ppermute | solution.py:494
  182.3 5.5 %shard_map.98 = bf16[512,1280]{1,0:T(8,128)(2,1)} custom-call(bf16[2560,1280]{1,0:T(8,128)(2,1)S(1)} %get-tuple-element.50.rows_ref, bf16[512,640]{1,0:T(8,128)(2,1)S(1)} %collective-permute-done.21.refs_0_, bf16[512,640]{1,0:T(8,128)(2,1)S(1)} %collective-permute-done.22.refs_1_, bf16[512,640]{1,0:T(8,128)(2,1)S(1)} %collective-permute-done.23.refs_2_, ...), custom_call_target="tpu_custom_call" | custom-call | flops 26843545600 | bytes 9175040 | tf_op jit(solution)/shard_map/pallas_call | solution.py:288
  (126 shorter events, 61.2 us)
Async XLA Ops:
  2.2 18.8 %collective-permute-start = (bf16[512,640]{1,0:T(8,128)(2,1)}, bf16[512,640]{1,0:T(8,128)(2,1)}, u32[]{:S(2)}, u32[]{:S(2)}) collective-permute-start(bf16[512,640]{1,0:T(8,128)(2,1)} %constant_dynamic-slice_fusion.2), channel_id=1, source_target_pairs={{0,4},{4,0},{8,12},{12,8},{16,20},{20,16},{24,28},{28,24},{1,5},{5... | collective-permute-start | bytes 1966088 | tf_op jit(solution)/shard_map/ppermute | solution.py:337
  5.1 29.1 %collective-permute-start.1 = (f32[512]{0:T(512)S(1)}, f32[512]{0:T(512)S(1)}, u32[]{:S(2)}, u32[]{:S(2)}) collective-permute-start(f32[512]{0:T(512)S(1)} %bitcast.39), channel_id=1, source_target_pairs={{0,4},{4,0},{8,12},{12,8},{16,20},{20,16},{24,28},{28,24},{1,5},{5... | collective-permute-start | bytes 6152 | tf_op jit(solution)/shard_map/ppermute | solution.py:337
  7.5 26.8 %collective-permute-start.2 = (bf16[512,640]{1,0:T(8,128)(2,1)}, bf16[512,640]{1,0:T(8,128)(2,1)}, u32[]{:S(2)}, u32[]{:S(2)}) collective-permute-start(bf16[512,640]{1,0:T(8,128)(2,1)} %get-tuple-element.71), channel_id=1, source_target_pairs={{0,4},{4,0},{8,12},{12,8},{16,20},{20,16},{24,28},{28,24},{1,5},{5... | collective-permute-start | bytes 1966088 | tf_op jit(solution)/shard_map/ppermute | solution.py:337
  23.2 16.8 %collective-permute-start.5 = (bf16[512,640]{1,0:T(8,128)(2,1)S(1)}, bf16[512,640]{1,0:T(8,128)(2,1)S(1)}, u32[]{:S(2)}, u32[]{:S(2)}) collective-permute-start(bf16[512,640]{1,0:T(8,128)(2,1)S(1)} %get-tuple-element.66), channel_id=1, source_target_pairs={{0,8},{4,12},{8,16},{12,20},{16,24},{20,28},{1,9},{5,13},{9,17},{1... | collective-permute-start | bytes 1966088 | tf_op jit(solution)/shard_map/ppermute | solution.py:340
  36.2 20.5 %collective-permute-start.3 = (bf16[640,640]{1,0:T(8,128)(2,1)S(1)}, bf16[640,640]{1,0:T(8,128)(2,1)S(1)}, u32[]{:S(2)}, u32[]{:S(2)}) collective-permute-start(bf16[640,640]{1,0:T(8,128)(2,1)S(1)} %get-tuple-element.79), channel_id=1, source_target_pairs={{0,8},{4,12},{24,16},{28,20},{25,17},{29,21},{1,9},{5,13},{2,10},{... | collective-permute-start | bytes 2457608 | tf_op jit(solution)/shard_map/ppermute | solution.py:354
  42.9 15.4 %collective-permute-start.6 = (bf16[512,640]{1,0:T(8,128)(2,1)S(1)}, bf16[512,640]{1,0:T(8,128)(2,1)S(1)}, u32[]{:S(2)}, u32[]{:S(2)}) collective-permute-start(bf16[512,640]{1,0:T(8,128)(2,1)S(1)} %get-tuple-element.39), channel_id=1, source_target_pairs={{8,16},{12,20},{16,24},{20,28},{9,17},{13,21},{17,25},{21,29},{10,... | collective-permute-start | bytes 1966088 | tf_op jit(solution)/shard_map/ppermute | solution.py:340
  59.2 21.5 %collective-permute-start.7 = (bf16[640,640]{1,0:T(8,128)(2,1)}, bf16[640,640]{1,0:T(8,128)(2,1)}, u32[]{:S(2)}, u32[]{:S(2)}) collective-permute-start(bf16[640,640]{1,0:T(8,128)(2,1)} %get-tuple-element.38), channel_id=1, source_target_pairs={{0,8},{4,12},{8,0},{12,4},{16,24},{20,28},{24,16},{28,20},{1,9},{5... | collective-permute-start | bytes 2457608 | tf_op jit(solution)/shard_map/ppermute | solution.py:340
  63.7 23.2 %collective-permute-start.8 = (bf16[640,640]{1,0:T(8,128)(2,1)}, bf16[640,640]{1,0:T(8,128)(2,1)}, u32[]{:S(2)}, u32[]{:S(2)}) collective-permute-start(bf16[640,640]{1,0:T(8,128)(2,1)} %get-tuple-element.61), channel_id=1, source_target_pairs={{16,8},{20,12},{9,17},{13,21},{18,10},{22,14},{11,19},{15,23}} | collective-permute-start | bytes 2457608 | tf_op jit(solution)/shard_map/ppermute | solution.py:354
  68.2 23.6 %collective-permute-start.9 = (bf16[512,640]{1,0:T(8,128)(2,1)S(1)}, bf16[512,640]{1,0:T(8,128)(2,1)S(1)}, u32[]{:S(2)}, u32[]{:S(2)}) collective-permute-start(bf16[512,640]{1,0:T(8,128)(2,1)S(1)} %copy-done.9), channel_id=1, source_target_pairs={{0,8},{4,12},{1,9},{5,13},{2,10},{6,14},{3,11},{7,15}} | collective-permute-start | bytes 1966088 | tf_op jit(solution)/shard_map/ppermute | solution.py:340
  82.8 21.9 %collective-permute-start.10 = (bf16[640,640]{1,0:T(8,128)(2,1)S(1)}, bf16[640,640]{1,0:T(8,128)(2,1)S(1)}, u32[]{:S(2)}, u32[]{:S(2)}) collective-permute-start(bf16[640,640]{1,0:T(8,128)(2,1)S(1)} %get-tuple-element.59), channel_id=1, source_target_pairs={{16,0},{20,4},{8,24},{12,28},{17,1},{21,5},{9,25},{13,29},{18,2},{... | collective-permute-start | bytes 2457608 | tf_op jit(solution)/shard_map/ppermute | solution.py:340
  85.3 30.9 %collective-permute-start.4 = (bf16[512,640]{1,0:T(8,128)(2,1)S(1)}, bf16[512,640]{1,0:T(8,128)(2,1)S(1)}, u32[]{:S(2)}, u32[]{:S(2)}) collective-permute-start(bf16[512,640]{1,0:T(8,128)(2,1)S(1)} %copy-done.17), channel_id=1, source_target_pairs={{0,4},{4,0},{8,12},{12,8},{16,20},{20,16},{24,28},{28,24},{1,5},{5... | collective-permute-start | bytes 1966088 | tf_op jit(solution)/shard_map/ppermute | solution.py:337
  104.9 29.3 %collective-permute-start.17 = (bf16[640,640]{1,0:T(8,128)(2,1)S(1)}, bf16[640,640]{1,0:T(8,128)(2,1)S(1)}, u32[]{:S(2)}, u32[]{:S(2)}) collective-permute-start(bf16[640,640]{1,0:T(8,128)(2,1)S(1)} %shard_map.91), channel_id=1, source_target_pairs={{8,16},{12,20},{17,9},{21,13},{10,18},{14,22},{19,11},{23,15}} | collective-permute-start | bytes 2457608 | tf_op jit(solution)/shard_map/ppermute | solution.py:354
  105.6 28.5 %collective-permute-start.16 = (bf16[640,640]{1,0:T(8,128)(2,1)S(1)}, bf16[640,640]{1,0:T(8,128)(2,1)S(1)}, u32[]{:S(2)}, u32[]{:S(2)}) collective-permute-start(bf16[640,640]{1,0:T(8,128)(2,1)S(1)} %shard_map.91), channel_id=1, source_target_pairs={{8,0},{12,4},{17,25},{21,29},{10,2},{14,6},{19,27},{23,31}} | collective-permute-start | bytes 2457608 | tf_op jit(solution)/shard_map/ppermute | solution.py:354
  114.7 11.3 %collective-permute-start.11 = (bf16[320,640]{1,0:T(8,128)(2,1)S(1)}, bf16[320,640]{1,0:T(8,128)(2,1)S(1)}, u32[]{:S(2)}, u32[]{:S(2)}) collective-permute-start(bf16[320,640]{1,0:T(8,128)(2,1)S(1)} %slice.8), channel_id=1, source_target_pairs={{0,16},{4,20},{24,8},{28,12},{1,17},{5,21},{25,9},{29,13},{2,18},{... | collective-permute-start | bytes 1228808 | tf_op jit(solution)/shard_map/ppermute | solution.py:340
  126.0 12.5 %collective-permute-start.12 = (bf16[320,640]{1,0:T(8,128)(2,1)S(1)}, bf16[320,640]{1,0:T(8,128)(2,1)S(1)}, u32[]{:S(2)}, u32[]{:S(2)}) collective-permute-start(bf16[320,640]{1,0:T(8,128)(2,1)S(1)} %get-tuple-element.74), channel_id=1, source_target_pairs={{0,16},{4,20},{24,8},{28,12},{1,17},{5,21},{25,9},{29,13},{2,18},{... | collective-permute-start | bytes 1228808 | tf_op jit(solution)/shard_map/ppermute | solution.py:340
  131.5 17.2 %collective-permute-start.13 = (bf16[640,640]{1,0:T(8,128)(2,1)S(1)}, bf16[640,640]{1,0:T(8,128)(2,1)S(1)}, u32[]{:S(2)}, u32[]{:S(2)}) collective-permute-start(bf16[640,640]{1,0:T(8,128)(2,1)S(1)} %shard_map.92), channel_id=1, source_target_pairs={{0,8},{4,12},{24,16},{28,20},{1,9},{5,13},{25,17},{29,21},{2,10},{... | collective-permute-start | bytes 2457608 | tf_op jit(solution)/shard_map/ppermute | solution.py:340
  132.8 15.0 %collective-permute-start.14 = (bf16[320,640]{1,0:T(8,128)(2,1)S(1)}, bf16[320,640]{1,0:T(8,128)(2,1)S(1)}, u32[]{:S(2)}, u32[]{:S(2)}) collective-permute-start(bf16[320,640]{1,0:T(8,128)(2,1)S(1)} %collective-permute-done.11), channel_id=1, source_target_pairs={{8,0},{12,4},{16,24},{20,28},{9,1},{13,5},{17,25},{21,29},{10,2},{... | collective-permute-start | bytes 1228808 | tf_op jit(solution)/shard_map/ppermute | solution.py:340
  134.3 14.7 %collective-permute-start.18 = (bf16[640,640]{1,0:T(8,128)(2,1)S(1)}, bf16[640,640]{1,0:T(8,128)(2,1)S(1)}, u32[]{:S(2)}, u32[]{:S(2)}) collective-permute-start(bf16[640,640]{1,0:T(8,128)(2,1)S(1)} %select_select_fusion), channel_id=1, source_target_pairs={{16,24},{20,28},{9,1},{13,5},{18,26},{22,30},{11,3},{15,7}} | collective-permute-start | bytes 2457608 | tf_op jit(solution)/shard_map/ppermute | solution.py:354
  138.6 10.0 %collective-permute-start.15 = (bf16[320,640]{1,0:T(8,128)(2,1)S(1)}, bf16[320,640]{1,0:T(8,128)(2,1)S(1)}, u32[]{:S(2)}, u32[]{:S(2)}) collective-permute-start(bf16[320,640]{1,0:T(8,128)(2,1)S(1)} %collective-permute-done.12), channel_id=1, source_target_pairs={{8,0},{12,4},{16,24},{20,28},{9,1},{13,5},{17,25},{21,29},{10,2},{... | collective-permute-start | bytes 1228808 | tf_op jit(solution)/shard_map/ppermute | solution.py:340
  154.2 10.7 %collective-permute-start.19 = (bf16[512,640]{1,0:T(8,128)(2,1)S(1)}, bf16[512,640]{1,0:T(8,128)(2,1)S(1)}, u32[]{:S(2)}, u32[]{:S(2)}) collective-permute-start(bf16[512,640]{1,0:T(8,128)(2,1)S(1)} %get-tuple-element.52), channel_id=1, source_target_pairs={{0,4},{4,0},{8,12},{12,8},{16,20},{20,16},{24,28},{28,24},{1,5},{5... | collective-permute-start | bytes 1966088 | tf_op jit(solution)/shard_map/ppermute | solution.py:337
  155.9 17.3 %collective-permute-start.20 = (bf16[512,640]{1,0:T(8,128)(2,1)S(1)}, bf16[512,640]{1,0:T(8,128)(2,1)S(1)}, u32[]{:S(2)}, u32[]{:S(2)}) collective-permute-start(bf16[512,640]{1,0:T(8,128)(2,1)S(1)} %get-tuple-element.53.after_ref.refs_0_), channel_id=1, source_target_pairs={{0,2},{1,3},{2,0},{3,1},{4,6},{5,7},{6,4},{7,5},{8,10},{9,11},{10,... | collective-permute-start | bytes 1966088 | tf_op jit(solution)/shard_map/ppermute | solution.py:494
  164.9 15.3 %collective-permute-start.24 = (bf16[512,640]{1,0:T(8,128)(2,1)S(1)}, bf16[512,640]{1,0:T(8,128)(2,1)S(1)}, u32[]{:S(2)}, u32[]{:S(2)}) collective-permute-start(bf16[512,640]{1,0:T(8,128)(2,1)S(1)} %collective-permute-done.19.refs_1_), channel_id=1, source_target_pairs={{0,2},{1,3},{2,0},{3,1},{4,6},{5,7},{6,4},{7,5},{8,10},{9,11},{10,... | collective-permute-start | bytes 1966088 | tf_op jit(solution)/shard_map/ppermute | solution.py:494
  176.9 5.2 %collective-permute-start.21 = (bf16[512,640]{1,0:T(8,128)(2,1)S(1)}, bf16[512,640]{1,0:T(8,128)(2,1)S(1)}, u32[]{:S(2)}, u32[]{:S(2)}) collective-permute-start(bf16[512,640]{1,0:T(8,128)(2,1)S(1)} %get-tuple-element.53.after_ref.refs_0_), channel_id=1, source_target_pairs={{0,1},{1,0},{2,3},{3,2},{4,5},{5,4},{6,7},{7,6},{8,9},{9,8},{10,11... | collective-permute-start | bytes 1966088 | tf_op jit(solution)/shard_map/ppermute | solution.py:494
  177.0 5.1 %collective-permute-start.22 = (bf16[512,640]{1,0:T(8,128)(2,1)S(1)}, bf16[512,640]{1,0:T(8,128)(2,1)S(1)}, u32[]{:S(2)}, u32[]{:S(2)}) collective-permute-start(bf16[512,640]{1,0:T(8,128)(2,1)S(1)} %collective-permute-done.19.refs_1_), channel_id=1, source_target_pairs={{0,1},{1,0},{2,3},{3,2},{4,5},{5,4},{6,7},{7,6},{8,9},{9,8},{10,11... | collective-permute-start | bytes 1966088 | tf_op jit(solution)/shard_map/ppermute | solution.py:494
  (26 other events, 151.6 us)

commit v2 on v1

--- a/solution.py
+++ b/solution.py
@@ -493,14 +493,14 @@
     def swapped(part, bit):
         return lax.ppermute(part, "head", [(i, i ^ bit) for i in range(columns_of)])
 
-    turns = list(range(1, group)) + [0]
+    turns = list(range(group))
     combined = apply_fast(
         all_asked, new_gate, new_lift, new_down, attended, gain, [(member - by) % group for by in turns]
     )
     arrived = [
-        (to_member(rows_of, group - by), (member + by) % group) for by, rows_of in zip(turns[:-1], combined)
+        (to_member(rows_of, group - by), (member + by) % group) for by, rows_of in zip(turns[1:], combined[1:])
     ]
-    combined = combined[-1]
+    combined = combined[0]
     arrived = [(combined, member)] + arrived
 
     spot = jnp.stack([head_place] + [head for _, head in arrived]).astype(jnp.int32)

time: 189 us -> 189 us (level)
  no operation moved by 1% of the time
where the time goes in v2:
time: 189 us; the launch traced here: 188 us
  waiting for transfers between devices  70.2 us (37%)
  starting transfers between devices  41.2 us (22%)
  Pallas kernels  33.8 us (18%)
  matrix products  17.2 us (9%)
  other arithmetic  14 us (7%)
  local copies, waits for them, and re-layouts  10.7 us (6%)
    ppermute x10, waiting for transfers between devices, between_planes(): lax.ppermute(array, 'ctx', [(a * group + m, b * group + m) for a, b in pa...  40.9 us
    ppermute x10, starting transfers between devices, between_planes(): lax.ppermute(array, 'ctx', [(a * group + m, b * group + m) for a, b in pa...  21.3 us
    dot_general x12, matrix products, mm(): return lax.dot_general(a, b, (dims, ((), ())), preferred_element_type=f32)  17.2 us
    ppermute x5, waiting for transfers between devices, to_member(): return lax.ppermute(array, 'ctx', pairs)  12.6 us
    pallas_call x3, Pallas kernels, project(): pl.pallas_call(functools.partial(project_kernel, count), out_shape=jax.Sh...  11.2 us
    ppermute x6, waiting for transfers between devices, swapped(): return lax.ppermute(part, 'head', [(i, i ^ bit) for i in range(columns_of)])  9.5 us
    ppermute x5, starting transfers between devices, by_side(): return lax.ppermute(array, ('ctx', 'head'), moves)  8.2 us
    ppermute x5, starting transfers between devices, to_member(): return lax.ppermute(array, 'ctx', pairs)  8.17 us
  transfers between devices with their start and end apart: 26, of which 13 were waited for; matrix products, arithmetic and copies ran while one was open for 19% of the time, Pallas kernels for 12%

profile of v2, /device:TPU:0, one launch (start us, length us, event | category | flops | bytes accessed | tf_op | source)
XLA Modules:
  0.0 187.8 jit_solution(11834600799986343912)
XLA Ops:
  2.2 3.0 %collective-permute-start = (bf16[512,640]{1,0:T(8,128)(2,1)}, bf16[512,640]{1,0:T(8,128)(2,1)}, u32[]{:S(2)}, u32[]{:S(2)}) collective-permute-start(bf16[512,640]{1,0:T(8,128)(2,1)} %constant_dynamic-slice_fusion.2), channel_id=1, source_target_pairs={{0,4},{4,0},{8,12},{12,8},{16,20},{20,16},{24,28},{28,24},{1,5},{5... | collective-permute-start | bytes 1966088 | tf_op jit(solution)/shard_map/ppermute | solution.py:337
  5.2 2.2 %constant_dynamic-slice_fusion = (bf16[512,640]{1,0:T(8,128)(2,1)}, bf16[512,640]{1,0:T(8,128)(2,1)S(1)}) fusion(bf16[512,1280]{1,0:T(8,128)(2,1)} %param.11, s32[]{:T(128)S(6)} %select_n.197, s32[]{:T(128)S(6)} %select_n.198), kind=kLoop, calls=%fused_computation.65 | loop fusion | bytes 2621448 | tf_op jit(solution)/shard_map/dynamic_slice | solution.py:357
  17.0 4.0 %collective-permute-done = bf16[512,640]{1,0:T(8,128)(2,1)} collective-permute-done((bf16[512,640]{1,0:T(8,128)(2,1)}, bf16[512,640]{1,0:T(8,128)(2,1)}, u32[]{:S(2)}, u32[]{:S(2)}) %collective-permute-start) | collective-permute-done | bytes 655392 | tf_op jit(solution)/shard_map/ppermute | solution.py:337
  23.2 4.1 %collective-permute-start.5 = (bf16[512,640]{1,0:T(8,128)(2,1)S(1)}, bf16[512,640]{1,0:T(8,128)(2,1)S(1)}, u32[]{:S(2)}, u32[]{:S(2)}) collective-permute-start(bf16[512,640]{1,0:T(8,128)(2,1)S(1)} %get-tuple-element.66), channel_id=1, source_target_pairs={{0,8},{4,12},{8,16},{12,20},{16,24},{20,28},{1,9},{5,13},{9,17},{1... | collective-permute-start | bytes 1966088 | tf_op jit(solution)/shard_map/ppermute | solution.py:340
  31.0 3.3 %collective-permute-done.2 = bf16[512,640]{1,0:T(8,128)(2,1)} collective-permute-done((bf16[512,640]{1,0:T(8,128)(2,1)}, bf16[512,640]{1,0:T(8,128)(2,1)}, u32[]{:S(2)}, u32[]{:S(2)}) %collective-permute-start.2) | collective-permute-done | bytes 655392 | tf_op jit(solution)/shard_map/ppermute | solution.py:337
  36.2 3.8 %collective-permute-start.3 = (bf16[640,640]{1,0:T(8,128)(2,1)S(1)}, bf16[640,640]{1,0:T(8,128)(2,1)S(1)}, u32[]{:S(2)}, u32[]{:S(2)}) collective-permute-start(bf16[640,640]{1,0:T(8,128)(2,1)S(1)} %get-tuple-element.79), channel_id=1, source_target_pairs={{0,8},{4,12},{24,16},{28,20},{25,17},{29,21},{1,9},{5,13},{2,10},{... | collective-permute-start | bytes 2457608 | tf_op jit(solution)/shard_map/ppermute | solution.py:354
  45.6 3.9 %select_convert_fusion = (bf16[640,640]{1,0:T(8,128)(2,1)}, f32[640,640]{1,0:T(8,128)}) fusion(f32[640,640]{1,0:T(8,128)S(1)} %convolution_add_fusion.1, pred[]{:T(512)S(6)} %eq.77, f32[640,640]{1,0:T(8,128)S(1)} %fusion.13, bf16[512,640]{1,0:T(8,128)(2,1)} %collective-permute-done, f32[512,640]{1,0:T(8,128)S(1)} %fusion.40, ...), kind=kOutput, calls=%fused_computation.3 | convolution fusion | flops 423526400 | bytes 10321921 | tf_op jit(solution)/shard_map/dot_general | solution.py:26
  49.5 7.2 %collective-permute-done.3 = bf16[640,640]{1,0:T(8,128)(2,1)S(1)} collective-permute-done((bf16[640,640]{1,0:T(8,128)(2,1)S(1)}, bf16[640,640]{1,0:T(8,128)(2,1)S(1)}, u32[]{:S(2)}, u32[]{:S(2)}) %collective-permute-start.3) | collective-permute-done | bytes 819232 | tf_op jit(solution)/shard_map/ppermute | solution.py:354
  59.2 2.5 %collective-permute-start.7 = (bf16[640,640]{1,0:T(8,128)(2,1)}, bf16[640,640]{1,0:T(8,128)(2,1)}, u32[]{:S(2)}, u32[]{:S(2)}) collective-permute-start(bf16[640,640]{1,0:T(8,128)(2,1)} %get-tuple-element.38), channel_id=1, source_target_pairs={{0,8},{4,12},{8,0},{12,4},{16,24},{20,28},{24,16},{28,20},{1,9},{5... | collective-permute-start | bytes 2457608 | tf_op jit(solution)/shard_map/ppermute | solution.py:340
  69.8 10.8 %collective-permute-done.7 = bf16[640,640]{1,0:T(8,128)(2,1)} collective-permute-done((bf16[640,640]{1,0:T(8,128)(2,1)}, bf16[640,640]{1,0:T(8,128)(2,1)}, u32[]{:S(2)}, u32[]{:S(2)}) %collective-permute-start.7) | collective-permute-done | bytes 819232 | tf_op jit(solution)/shard_map/ppermute | solution.py:340
  88.2 3.5 %collective-permute-done.9 = bf16[512,640]{1,0:T(8,128)(2,1)S(1)} collective-permute-done((bf16[512,640]{1,0:T(8,128)(2,1)S(1)}, bf16[512,640]{1,0:T(8,128)(2,1)S(1)}, u32[]{:S(2)}, u32[]{:S(2)}) %collective-permute-start.9) | collective-permute-done | bytes 655392 | tf_op jit(solution)/shard_map/ppermute | solution.py:340
  91.8 12.9 %collective-permute-done.10 = bf16[640,640]{1,0:T(8,128)(2,1)S(1)} collective-permute-done((bf16[640,640]{1,0:T(8,128)(2,1)S(1)}, bf16[640,640]{1,0:T(8,128)(2,1)S(1)}, u32[]{:S(2)}, u32[]{:S(2)}) %collective-permute-start.10) | collective-permute-done | bytes 819232 | tf_op jit(solution)/shard_map/ppermute | solution.py:340
  106.9 7.7 %shard_map.92 = bf16[640,640]{1,0:T(8,128)(2,1)S(1)} custom-call(s32[1]{0:T(128)} %bitcast.9.active_ref, f32[640,640]{1,0:T(8,128)S(1)} %convert_add_fusion.grad_ref, bf16[640,640]{1,0:T(8,128)(2,1)S(1)} %bitcast_select_fusion.init_ref), custom_call_target="tpu_custom_call" | custom-call | flops 4718592000 | bytes 3276800 | tf_op jit(solution)/shard_map/pallas_call | solution.py:177
  116.6 9.4 %collective-permute-done.11 = bf16[320,640]{1,0:T(8,128)(2,1)S(1)} collective-permute-done((bf16[320,640]{1,0:T(8,128)(2,1)S(1)}, bf16[320,640]{1,0:T(8,128)(2,1)S(1)}, u32[]{:S(2)}, u32[]{:S(2)}) %collective-permute-start.11) | collective-permute-done | bytes 409632 | tf_op jit(solution)/shard_map/ppermute | solution.py:340
  126.0 5.3 %collective-permute-start.12 = (bf16[320,640]{1,0:T(8,128)(2,1)S(1)}, bf16[320,640]{1,0:T(8,128)(2,1)S(1)}, u32[]{:S(2)}, u32[]{:S(2)}) collective-permute-start(bf16[320,640]{1,0:T(8,128)(2,1)S(1)} %get-tuple-element.74), channel_id=1, source_target_pairs={{0,16},{4,20},{24,8},{28,12},{1,17},{5,21},{25,9},{29,13},{2,18},{... | collective-permute-start | bytes 1228808 | tf_op jit(solution)/shard_map/ppermute | solution.py:340
  135.0 3.6 %collective-permute-done.12 = bf16[320,640]{1,0:T(8,128)(2,1)S(1)} collective-permute-done((bf16[320,640]{1,0:T(8,128)(2,1)S(1)}, bf16[320,640]{1,0:T(8,128)(2,1)S(1)}, u32[]{:S(2)}, u32[]{:S(2)}) %collective-permute-start.12) | collective-permute-done | bytes 409632 | tf_op jit(solution)/shard_map/ppermute | solution.py:340
  140.2 7.6 %shard_map.93.att_ref = f32[1024,640]{1,0:T(8,128)S(1)} custom-call(s32[1]{0:T(128)} %bitcast.12.first_ref, bf16[1024,640]{1,0:T(8,128)(2,1)S(1)} %pad_maximum_fusion.q_ref, bf16[512,640]{1,0:T(8,128)(2,1)S(1)} %collective-permute-done.5.kp_ref, bf16[1024,640]{1,0:T(8,128)(2,1)S(1)} %pad_maximum_fusion.1.k_ref, ...), custom_call_target="tpu_custom_call" | custom-call | flops 1677721600 | bytes 7864320 | tf_op jit(solution)/shard_map/pallas_call | solution.py:123
  149.2 5.0 %shard_map.94 = (bf16[512,640]{1,0:T(8,128)(2,1)S(1)}, bf16[512,640]{1,0:T(8,128)(2,1)S(1)}) custom-call(s32[2]{0:T(128)S(1)} %pad_add_fusion.1.which_ref, bf16[1024,640]{1,0:T(8,128)(2,1)S(1)} %pad_maximum_fusion.q_ref, bf16[640,640]{1,0:T(8,128)(2,1)S(1)} %get-tuple-element.64.gate_ref, bf16[640,640]{1,0:T(8,128)(2,1)S(1)} %get-tuple-element.63.lift_ref, ...), custom_call_target="tpu_custom_call" | custom-call | flops 2516582400 | bytes 9011200 | tf_op jit(solution)/shard_map/pallas_call | solution.py:213
  157.3 2.2 %shard_map.95 = (bf16[1920,1280]{1,0:T(8,128)(2,1)S(1)}, bf16[640,1280]{1,0:T(8,128)(2,1)S(1)}, bf16[2560,1280]{1,0:T(8,128)(2,1)S(1)}) custom-call(s32[3]{0:T(128)S(1)} %pad_add_fusion.spot_ref, bf16[5120,1280]{1,0:T(8,128)(2,1)S(1)} %bitcast.36, bf16[512,640]{1,0:T(8,128)(2,1)S(1)} %get-tuple-element.53.after_ref.refs_0_), custom_call_target="tpu_custom_call" | custom-call | flops 10000000000 | bytes 26214400 | tf_op jit(solution)/shard_map/pallas_call | solution.py:251
  159.6 5.3 %collective-permute-done.19.refs_1_ = bf16[512,640]{1,0:T(8,128)(2,1)S(1)} collective-permute-done((bf16[512,640]{1,0:T(8,128)(2,1)S(1)}, bf16[512,640]{1,0:T(8,128)(2,1)S(1)}, u32[]{:S(2)}, u32[]{:S(2)}) %collective-permute-start.19) | collective-permute-done | bytes 655392 | tf_op jit(solution)/shard_map/ppermute | solution.py:337
  166.4 6.7 %collective-permute-done.20.refs_2_ = bf16[512,640]{1,0:T(8,128)(2,1)S(1)} collective-permute-done((bf16[512,640]{1,0:T(8,128)(2,1)S(1)}, bf16[512,640]{1,0:T(8,128)(2,1)S(1)}, u32[]{:S(2)}, u32[]{:S(2)}) %collective-permute-start.20) | collective-permute-done | bytes 655392 | tf_op jit(solution)/shard_map/ppermute | solution.py:494
  173.1 3.7 %shard_map.96.refs_1_ = f32[512,1280]{1,0:T(8,128)S(1)} custom-call(bf16[1920,1280]{1,0:T(8,128)(2,1)S(1)} %get-tuple-element.51.rows_ref, bf16[512,640]{1,0:T(8,128)(2,1)S(1)} %get-tuple-element.53.after_ref.refs_0_, bf16[512,640]{1,0:T(8,128)(2,1)S(1)} %collective-permute-done.19.refs_1_, bf16[512,640]{1,0:T(8,128)(2,1)S(1)} %collective-permute-done.20.refs_2_), custom_call_target="tpu_custom_call" | custom-call | flops 20132659200 | bytes 6881280 | tf_op jit(solution)/shard_map/pallas_call | solution.py:288
  177.5 2.6 %collective-permute-done.24.refs_0_ = bf16[512,640]{1,0:T(8,128)(2,1)S(1)} collective-permute-done((bf16[512,640]{1,0:T(8,128)(2,1)S(1)}, bf16[512,640]{1,0:T(8,128)(2,1)S(1)}, u32[]{:S(2)}, u32[]{:S(2)}) %collective-permute-start.24) | collective-permute-done | bytes 655392 | tf_op jit(solution)/shard_map/ppermute | solution.py:494
  182.3 5.5 %shard_map.98 = bf16[512,1280]{1,0:T(8,128)(2,1)} custom-call(bf16[2560,1280]{1,0:T(8,128)(2,1)S(1)} %get-tuple-element.50.rows_ref, bf16[512,640]{1,0:T(8,128)(2,1)S(1)} %collective-permute-done.21.refs_0_, bf16[512,640]{1,0:T(8,128)(2,1)S(1)} %collective-permute-done.22.refs_1_, bf16[512,640]{1,0:T(8,128)(2,1)S(1)} %collective-permute-done.23.refs_2_, ...), custom_call_target="tpu_custom_call" | custom-call | flops 26843545600 | bytes 9175040 | tf_op jit(solution)/shard_map/pallas_call | solution.py:288
  (126 shorter events, 61.2 us)
Async XLA Ops:
  2.2 18.8 %collective-permute-start = (bf16[512,640]{1,0:T(8,128)(2,1)}, bf16[512,640]{1,0:T(8,128)(2,1)}, u32[]{:S(2)}, u32[]{:S(2)}) collective-permute-start(bf16[512,640]{1,0:T(8,128)(2,1)} %constant_dynamic-slice_fusion.2), channel_id=1, source_target_pairs={{0,4},{4,0},{8,12},{12,8},{16,20},{20,16},{24,28},{28,24},{1,5},{5... | collective-permute-start | bytes 1966088 | tf_op jit(solution)/shard_map/ppermute | solution.py:337
  5.1 29.1 %collective-permute-start.1 = (f32[512]{0:T(512)S(1)}, f32[512]{0:T(512)S(1)}, u32[]{:S(2)}, u32[]{:S(2)}) collective-permute-start(f32[512]{0:T(512)S(1)} %bitcast.39), channel_id=1, source_target_pairs={{0,4},{4,0},{8,12},{12,8},{16,20},{20,16},{24,28},{28,24},{1,5},{5... | collective-permute-start | bytes 6152 | tf_op jit(solution)/shard_map/ppermute | solution.py:337
  7.5 26.8 %collective-permute-start.2 = (bf16[512,640]{1,0:T(8,128)(2,1)}, bf16[512,640]{1,0:T(8,128)(2,1)}, u32[]{:S(2)}, u32[]{:S(2)}) collective-permute-start(bf16[512,640]{1,0:T(8,128)(2,1)} %get-tuple-element.71), channel_id=1, source_target_pairs={{0,4},{4,0},{8,12},{12,8},{16,20},{20,16},{24,28},{28,24},{1,5},{5... | collective-permute-start | bytes 1966088 | tf_op jit(solution)/shard_map/ppermute | solution.py:337
  23.2 16.8 %collective-permute-start.5 = (bf16[512,640]{1,0:T(8,128)(2,1)S(1)}, bf16[512,640]{1,0:T(8,128)(2,1)S(1)}, u32[]{:S(2)}, u32[]{:S(2)}) collective-permute-start(bf16[512,640]{1,0:T(8,128)(2,1)S(1)} %get-tuple-element.66), channel_id=1, source_target_pairs={{0,8},{4,12},{8,16},{12,20},{16,24},{20,28},{1,9},{5,13},{9,17},{1... | collective-permute-start | bytes 1966088 | tf_op jit(solution)/shard_map/ppermute | solution.py:340
  36.2 20.5 %collective-permute-start.3 = (bf16[640,640]{1,0:T(8,128)(2,1)S(1)}, bf16[640,640]{1,0:T(8,128)(2,1)S(1)}, u32[]{:S(2)}, u32[]{:S(2)}) collective-permute-start(bf16[640,640]{1,0:T(8,128)(2,1)S(1)} %get-tuple-element.79), channel_id=1, source_target_pairs={{0,8},{4,12},{24,16},{28,20},{25,17},{29,21},{1,9},{5,13},{2,10},{... | collective-permute-start | bytes 2457608 | tf_op jit(solution)/shard_map/ppermute | solution.py:354
  42.9 15.4 %collective-permute-start.6 = (bf16[512,640]{1,0:T(8,128)(2,1)S(1)}, bf16[512,640]{1,0:T(8,128)(2,1)S(1)}, u32[]{:S(2)}, u32[]{:S(2)}) collective-permute-start(bf16[512,640]{1,0:T(8,128)(2,1)S(1)} %get-tuple-element.39), channel_id=1, source_target_pairs={{8,16},{12,20},{16,24},{20,28},{9,17},{13,21},{17,25},{21,29},{10,... | collective-permute-start | bytes 1966088 | tf_op jit(solution)/shard_map/ppermute | solution.py:340
  59.2 21.5 %collective-permute-start.7 = (bf16[640,640]{1,0:T(8,128)(2,1)}, bf16[640,640]{1,0:T(8,128)(2,1)}, u32[]{:S(2)}, u32[]{:S(2)}) collective-permute-start(bf16[640,640]{1,0:T(8,128)(2,1)} %get-tuple-element.38), channel_id=1, source_target_pairs={{0,8},{4,12},{8,0},{12,4},{16,24},{20,28},{24,16},{28,20},{1,9},{5... | collective-permute-start | bytes 2457608 | tf_op jit(solution)/shard_map/ppermute | solution.py:340
  63.7 23.2 %collective-permute-start.8 = (bf16[640,640]{1,0:T(8,128)(2,1)}, bf16[640,640]{1,0:T(8,128)(2,1)}, u32[]{:S(2)}, u32[]{:S(2)}) collective-permute-start(bf16[640,640]{1,0:T(8,128)(2,1)} %get-tuple-element.61), channel_id=1, source_target_pairs={{16,8},{20,12},{9,17},{13,21},{18,10},{22,14},{11,19},{15,23}} | collective-permute-start | bytes 2457608 | tf_op jit(solution)/shard_map/ppermute | solution.py:354
  68.2 23.6 %collective-permute-start.9 = (bf16[512,640]{1,0:T(8,128)(2,1)S(1)}, bf16[512,640]{1,0:T(8,128)(2,1)S(1)}, u32[]{:S(2)}, u32[]{:S(2)}) collective-permute-start(bf16[512,640]{1,0:T(8,128)(2,1)S(1)} %copy-done.9), channel_id=1, source_target_pairs={{0,8},{4,12},{1,9},{5,13},{2,10},{6,14},{3,11},{7,15}} | collective-permute-start | bytes 1966088 | tf_op jit(solution)/shard_map/ppermute | solution.py:340
  82.8 21.9 %collective-permute-start.10 = (bf16[640,640]{1,0:T(8,128)(2,1)S(1)}, bf16[640,640]{1,0:T(8,128)(2,1)S(1)}, u32[]{:S(2)}, u32[]{:S(2)}) collective-permute-start(bf16[640,640]{1,0:T(8,128)(2,1)S(1)} %get-tuple-element.59), channel_id=1, source_target_pairs={{16,0},{20,4},{8,24},{12,28},{17,1},{21,5},{9,25},{13,29},{18,2},{... | collective-permute-start | bytes 2457608 | tf_op jit(solution)/shard_map/ppermute | solution.py:340
  85.3 30.9 %collective-permute-start.4 = (bf16[512,640]{1,0:T(8,128)(2,1)S(1)}, bf16[512,640]{1,0:T(8,128)(2,1)S(1)}, u32[]{:S(2)}, u32[]{:S(2)}) collective-permute-start(bf16[512,640]{1,0:T(8,128)(2,1)S(1)} %copy-done.17), channel_id=1, source_target_pairs={{0,4},{4,0},{8,12},{12,8},{16,20},{20,16},{24,28},{28,24},{1,5},{5... | collective-permute-start | bytes 1966088 | tf_op jit(solution)/shard_map/ppermute | solution.py:337
  104.9 29.3 %collective-permute-start.17 = (bf16[640,640]{1,0:T(8,128)(2,1)S(1)}, bf16[640,640]{1,0:T(8,128)(2,1)S(1)}, u32[]{:S(2)}, u32[]{:S(2)}) collective-permute-start(bf16[640,640]{1,0:T(8,128)(2,1)S(1)} %shard_map.91), channel_id=1, source_target_pairs={{8,16},{12,20},{17,9},{21,13},{10,18},{14,22},{19,11},{23,15}} | collective-permute-start | bytes 2457608 | tf_op jit(solution)/shard_map/ppermute | solution.py:354
  105.6 28.5 %collective-permute-start.16 = (bf16[640,640]{1,0:T(8,128)(2,1)S(1)}, bf16[640,640]{1,0:T(8,128)(2,1)S(1)}, u32[]{:S(2)}, u32[]{:S(2)}) collective-permute-start(bf16[640,640]{1,0:T(8,128)(2,1)S(1)} %shard_map.91), channel_id=1, source_target_pairs={{8,0},{12,4},{17,25},{21,29},{10,2},{14,6},{19,27},{23,31}} | collective-permute-start | bytes 2457608 | tf_op jit(solution)/shard_map/ppermute | solution.py:354
  114.7 11.3 %collective-permute-start.11 = (bf16[320,640]{1,0:T(8,128)(2,1)S(1)}, bf16[320,640]{1,0:T(8,128)(2,1)S(1)}, u32[]{:S(2)}, u32[]{:S(2)}) collective-permute-start(bf16[320,640]{1,0:T(8,128)(2,1)S(1)} %slice.8), channel_id=1, source_target_pairs={{0,16},{4,20},{24,8},{28,12},{1,17},{5,21},{25,9},{29,13},{2,18},{... | collective-permute-start | bytes 1228808 | tf_op jit(solution)/shard_map/ppermute | solution.py:340
  126.0 12.5 %collective-permute-start.12 = (bf16[320,640]{1,0:T(8,128)(2,1)S(1)}, bf16[320,640]{1,0:T(8,128)(2,1)S(1)}, u32[]{:S(2)}, u32[]{:S(2)}) collective-permute-start(bf16[320,640]{1,0:T(8,128)(2,1)S(1)} %get-tuple-element.74), channel_id=1, source_target_pairs={{0,16},{4,20},{24,8},{28,12},{1,17},{5,21},{25,9},{29,13},{2,18},{... | collective-permute-start | bytes 1228808 | tf_op jit(solution)/shard_map/ppermute | solution.py:340
  131.5 17.2 %collective-permute-start.13 = (bf16[640,640]{1,0:T(8,128)(2,1)S(1)}, bf16[640,640]{1,0:T(8,128)(2,1)S(1)}, u32[]{:S(2)}, u32[]{:S(2)}) collective-permute-start(bf16[640,640]{1,0:T(8,128)(2,1)S(1)} %shard_map.92), channel_id=1, source_target_pairs={{0,8},{4,12},{24,16},{28,20},{1,9},{5,13},{25,17},{29,21},{2,10},{... | collective-permute-start | bytes 2457608 | tf_op jit(solution)/shard_map/ppermute | solution.py:340
  132.8 15.0 %collective-permute-start.14 = (bf16[320,640]{1,0:T(8,128)(2,1)S(1)}, bf16[320,640]{1,0:T(8,128)(2,1)S(1)}, u32[]{:S(2)}, u32[]{:S(2)}) collective-permute-start(bf16[320,640]{1,0:T(8,128)(2,1)S(1)} %collective-permute-done.11), channel_id=1, source_target_pairs={{8,0},{12,4},{16,24},{20,28},{9,1},{13,5},{17,25},{21,29},{10,2},{... | collective-permute-start | bytes 1228808 | tf_op jit(solution)/shard_map/ppermute | solution.py:340
  134.3 14.7 %collective-permute-start.18 = (bf16[640,640]{1,0:T(8,128)(2,1)S(1)}, bf16[640,640]{1,0:T(8,128)(2,1)S(1)}, u32[]{:S(2)}, u32[]{:S(2)}) collective-permute-start(bf16[640,640]{1,0:T(8,128)(2,1)S(1)} %select_select_fusion), channel_id=1, source_target_pairs={{16,24},{20,28},{9,1},{13,5},{18,26},{22,30},{11,3},{15,7}} | collective-permute-start | bytes 2457608 | tf_op jit(solution)/shard_map/ppermute | solution.py:354
  138.6 10.0 %collective-permute-start.15 = (bf16[320,640]{1,0:T(8,128)(2,1)S(1)}, bf16[320,640]{1,0:T(8,128)(2,1)S(1)}, u32[]{:S(2)}, u32[]{:S(2)}) collective-permute-start(bf16[320,640]{1,0:T(8,128)(2,1)S(1)} %collective-permute-done.12), channel_id=1, source_target_pairs={{8,0},{12,4},{16,24},{20,28},{9,1},{13,5},{17,25},{21,29},{10,2},{... | collective-permute-start | bytes 1228808 | tf_op jit(solution)/shard_map/ppermute | solution.py:340
  154.2 10.7 %collective-permute-start.19 = (bf16[512,640]{1,0:T(8,128)(2,1)S(1)}, bf16[512,640]{1,0:T(8,128)(2,1)S(1)}, u32[]{:S(2)}, u32[]{:S(2)}) collective-permute-start(bf16[512,640]{1,0:T(8,128)(2,1)S(1)} %get-tuple-element.52), channel_id=1, source_target_pairs={{0,4},{4,0},{8,12},{12,8},{16,20},{20,16},{24,28},{28,24},{1,5},{5... | collective-permute-start | bytes 1966088 | tf_op jit(solution)/shard_map/ppermute | solution.py:337
  155.9 17.3 %collective-permute-start.20 = (bf16[512,640]{1,0:T(8,128)(2,1)S(1)}, bf16[512,640]{1,0:T(8,128)(2,1)S(1)}, u32[]{:S(2)}, u32[]{:S(2)}) collective-permute-start(bf16[512,640]{1,0:T(8,128)(2,1)S(1)} %get-tuple-element.53.after_ref.refs_0_), channel_id=1, source_target_pairs={{0,2},{1,3},{2,0},{3,1},{4,6},{5,7},{6,4},{7,5},{8,10},{9,11},{10,... | collective-permute-start | bytes 1966088 | tf_op jit(solution)/shard_map/ppermute | solution.py:494
  164.9 15.3 %collective-permute-start.24 = (bf16[512,640]{1,0:T(8,128)(2,1)S(1)}, bf16[512,640]{1,0:T(8,128)(2,1)S(1)}, u32[]{:S(2)}, u32[]{:S(2)}) collective-permute-start(bf16[512,640]{1,0:T(8,128)(2,1)S(1)} %collective-permute-done.19.refs_1_), channel_id=1, source_target_pairs={{0,2},{1,3},{2,0},{3,1},{4,6},{5,7},{6,4},{7,5},{8,10},{9,11},{10,... | collective-permute-start | bytes 1966088 | tf_op jit(solution)/shard_map/ppermute | solution.py:494
  176.9 5.2 %collective-permute-start.21 = (bf16[512,640]{1,0:T(8,128)(2,1)S(1)}, bf16[512,640]{1,0:T(8,128)(2,1)S(1)}, u32[]{:S(2)}, u32[]{:S(2)}) collective-permute-start(bf16[512,640]{1,0:T(8,128)(2,1)S(1)} %get-tuple-element.53.after_ref.refs_0_), channel_id=1, source_target_pairs={{0,1},{1,0},{2,3},{3,2},{4,5},{5,4},{6,7},{7,6},{8,9},{9,8},{10,11... | collective-permute-start | bytes 1966088 | tf_op jit(solution)/shard_map/ppermute | solution.py:494
  177.0 5.1 %collective-permute-start.22 = (bf16[512,640]{1,0:T(8,128)(2,1)S(1)}, bf16[512,640]{1,0:T(8,128)(2,1)S(1)}, u32[]{:S(2)}, u32[]{:S(2)}) collective-permute-start(bf16[512,640]{1,0:T(8,128)(2,1)S(1)} %collective-permute-done.19.refs_1_), channel_id=1, source_target_pairs={{0,1},{1,0},{2,3},{3,2},{4,5},{5,4},{6,7},{7,6},{8,9},{9,8},{10,11... | collective-permute-start | bytes 1966088 | tf_op jit(solution)/shard_map/ppermute | solution.py:494
  (26 other events, 151.6 us)
